TPU v7x, 32 devices: a whole 2x2x4 slice. The times are simulated.
32 devices in a mesh: prod: 4 (over y, x), cand: 8 (over z, core).
Axes of the slice: x: 2, y: 2, z: 4, core: 2. Of those that a mesh axis runs over, the one named last changes fastest.
Arguments:
- cand_states: bfloat16 [4, 8, 128, 4096], P('prod', 'cand'), may hold values from -600 to 600
- enc_rows: bfloat16 [4, 256, 4096], P('prod', 'cand'), may hold values from -120 to 120
- w_query: bfloat16 [4096, 4096], P('prod', 'cand'), may hold values from -0.09375 to 0.09375
- w_key: bfloat16 [4096, 4096], P('prod', 'cand'), may hold values from -0.09375 to 0.09375
- w_value: bfloat16 [4096, 4096], P('prod', 'cand'), may hold values from -0.09375 to 0.09375
- w_out: bfloat16 [4096, 4096], P('cand', 'prod'), may hold values from -0.375 to 0.375
- tile_mask: int32 [4, 8, 2], P('prod', 'cand'), may hold values from 0 to 1, as said below
- counts: int32 [4], P('prod'), may hold values from 1 to 8, as said below
Outputs:
- cross_out: bfloat16 [4, 8, 128, 4096], P('prod', 'cand')
Inputs may be any that keep to these rules, and one draw needn't show every extreme that they name: `tile_mask`: every candidate has at least one tile set. `counts`: some product fills all 8 slots.
All inputs are finite; a program needn't handle non-finite values.
Results may differ from a plain program's by a relative error of at most 0.023.
The roundings to bfloat16 on the way count: a program that leaves them out, or rounds other values in their place, can miss the bound.
Values may be sent and summed in bfloat16 or wider, within the bound.
No kernel may reach another device: no remote copies, remote signals or barrier semaphores. Data moves between devices by JAX's collectives and lax.ppermute only.
A program may use at most 128 MiB of HBM per device.

v0:
```python
import functools

import jax
import jax.numpy as jnp
from jax import lax
from jax.experimental import pallas as pl
from jax.experimental.pallas import tpu as pltpu
from jax.sharding import PartitionSpec as P

HD = 64
TILE = 128
LANES = 128
FLAG_ROWS = 16
VMEM = pltpu.CompilerParams(vmem_limit_bytes=40 * 1024 * 1024)


def ring_order(chips):
    odd = list(range(1, chips, 2))
    even = list(range(2, chips, 2))
    return [0] + odd + even[::-1]


def small():
    return pl.CostEstimate(flops=1, bytes_accessed=1, transcendentals=0)


def columns_kernel(ids, x_ref, *outs):
    block = outs[0].shape[1]
    for r, out in enumerate(outs):
        source = jnp.bitwise_xor(ids[0], r)
        out[...] = x_ref[:, pl.ds(pl.multiple_of(source * block, block), block)]


def column_blocks(ids, x, parts):
    shape = jax.ShapeDtypeStruct((x.shape[0], x.shape[1] // parts), x.dtype)
    return pl.pallas_call(
        columns_kernel,
        out_shape=[shape] * parts,
        in_specs=[
            pl.BlockSpec(memory_space=pltpu.SMEM),
            pl.BlockSpec(memory_space=pltpu.VMEM),
        ],
        out_specs=[pl.BlockSpec(memory_space=pltpu.VMEM)] * parts,
        compiler_params=VMEM,
        cost_estimate=small(),
        name="columns",
    )(ids, x)


def key_value_kernel(parts, rows, tiles, tile_of, enc_ref, w_key, w_value, open_ref, *outs):
    slots, height, block = enc_ref.shape
    local = w_key.shape[1]
    encoder = jnp.concatenate([enc_ref[slot, : parts * rows, :] for slot in range(slots)], axis=0)
    for column, weight in ((0, w_key), (local, w_value)):
        sums = jnp.dot(encoder, weight[...], preferred_element_type=jnp.float32)
        for slot in range(slots):
            for r in range(parts):
                start = (slot * parts + r) * rows
                outs[r][slot * rows : (slot + 1) * rows, column : column + local] = sums[
                    start : start + rows
                ].astype(outs[r].dtype)
    elen = slots * rows
    tile = lax.broadcasted_iota(jnp.int32, (1, elen), 1) // tile_of
    for slot in range(slots):
        seen = jnp.zeros((1, elen), jnp.float32)
        for t in range(tiles):
            start = t * (block // tiles)
            flag = enc_ref[slot, height - 1 : height, start : start + elen].astype(jnp.float32)
            seen = jnp.where(tile == t, flag, seen)
        open_ref[slot : slot + 1, :] = seen


def key_value(gathered, w_key, w_value, parts, rows, tiles):
    slots, local = gathered.shape[0], w_key.shape[1]
    elen = slots * rows
    return pl.pallas_call(
        functools.partial(key_value_kernel, parts, rows, tiles, TILE),
        out_shape=[jax.ShapeDtypeStruct((slots, elen), jnp.float32)]
        + [
            jax.ShapeDtypeStruct((elen, 2 * local), jnp.float32 if r == 0 else jnp.bfloat16)
            for r in range(parts)
        ],
        in_specs=[pl.BlockSpec(memory_space=pltpu.VMEM)] * 3,
        out_specs=[pl.BlockSpec(memory_space=pltpu.VMEM)] * (parts + 1),
        compiler_params=VMEM,
        cost_estimate=small(),
        name="key_value",
    )(gathered, w_key, w_value)


def query_kernel(pieces, parts, ids, mine, sib, *refs):
    weights, out_ref = refs[:pieces], refs[pieces]
    clen, width = mine.shape
    block = width // parts
    scales = []
    for ref in (mine, sib):
        values = ref[...].astype(jnp.float32)
        scales.append(lax.rsqrt(jnp.sum(values * values, axis=-1, keepdims=True) / width + 1e-06))
    total, start = None, 0
    for weight in weights:
        depth = weight.shape[0]
        from_prod = jnp.bitwise_xor(ids[0], start // block)
        source = pl.multiple_of(from_prod * block + start % block, LANES)
        rows = jnp.concatenate(
            [
                (ref[:, pl.ds(source, depth)].astype(jnp.float32) * scale).astype(jnp.bfloat16)
                for ref, scale in zip((mine, sib), scales)
            ],
            axis=0,
        )
        term = jnp.dot(rows, weight[...], preferred_element_type=jnp.float32)
        total = term if total is None else total + term
        start += depth
    out_ref[...] = total.astype(jnp.bfloat16)


def query(ids, mine, sib, weights, parts):
    clen = mine.shape[0]
    return pl.pallas_call(
        functools.partial(query_kernel, len(weights), parts),
        out_shape=jax.ShapeDtypeStruct((2 * clen, weights[0].shape[1]), jnp.bfloat16),
        in_specs=[pl.BlockSpec(memory_space=pltpu.SMEM)]
        + [pl.BlockSpec(memory_space=pltpu.VMEM)] * (2 + len(weights)),
        out_specs=pl.BlockSpec(memory_space=pltpu.VMEM),
        compiler_params=VMEM,
        cost_estimate=small(),
        name="query",
    )(ids, mine, sib, *weights)


def attend_kernel(order, step, ids, query_ref, open_ref, kv_ref, out_ref):
    chips = len(order)
    chip, core = lax.div(ids[1], 2), lax.rem(ids[1], 2)
    source = chip
    if step:
        for place in range(chips):
            source = jnp.where(chip == order[place], order[(place - step) % chips], source)
    who = (2 * source + core, 2 * source + 1 - core)
    clen = query_ref.shape[0] // 2
    elen, local = kv_ref.shape[0], kv_ref.shape[1] // 2
    is_open = (
        jnp.concatenate(
            [jnp.broadcast_to(open_ref[pl.ds(who[i], 1), :], (clen, elen)) for i in range(2)],
            axis=0,
        )
        > 0.5
    )
    lane = lax.broadcasted_iota(jnp.int32, (elen, LANES), 1) // HD
    for pair in range(local // LANES):
        columns = slice(pair * LANES, (pair + 1) * LANES)
        keys = kv_ref[:, columns]
        values = kv_ref[:, local + pair * LANES : local + (pair + 1) * LANES]
        context = None
        for half in range(LANES // HD):
            own = lane == half
            scores = (
                lax.dot_general(
                    query_ref[:, columns],
                    jnp.where(own, keys, jnp.zeros_like(keys)),
                    (((1,), (1,)), ((), ())),
                    preferred_element_type=jnp.float32,
                )
                * 0.125
            )
            scores = jnp.where(is_open, scores, -1e30)
            top = jnp.max(scores, axis=-1, keepdims=True)
            grown = jnp.exp(scores - top)
            probs = (grown / jnp.sum(grown, axis=-1, keepdims=True)).astype(jnp.bfloat16)
            term = jnp.dot(
                probs,
                jnp.where(own, values, jnp.zeros_like(values)),
                preferred_element_type=jnp.float32,
            )
            context = term if context is None else context + term
        out_ref[:, columns] = context.astype(jnp.bfloat16)


def attend(order, step, ids, queries, is_open, kv):
    return pl.pallas_call(
        functools.partial(attend_kernel, order, step),
        out_shape=jax.ShapeDtypeStruct(queries.shape, jnp.bfloat16),
        in_specs=[pl.BlockSpec(memory_space=pltpu.SMEM)]
        + [pl.BlockSpec(memory_space=pltpu.VMEM)] * 3,
        out_specs=pl.BlockSpec(memory_space=pltpu.VMEM),
        compiler_params=VMEM,
        cost_estimate=small(),
        name="attend",
    )(ids, queries, is_open, kv)


def project_kernel(pieces, context_ref, *refs):
    weights, (mine, sib) = refs[: len(pieces)], refs[len(pieces) :]
    clen = mine.shape[0]
    totals = {}
    for (r, row), weight in zip(pieces, weights):
        term = jnp.dot(
            context_ref[:, row : row + weight.shape[0]],
            weight[...],
            preferred_element_type=jnp.float32,
        )
        totals[r] = term if r not in totals else totals[r] + term
        if row + weight.shape[0] == context_ref.shape[1]:
            block = weight.shape[1]
            rows = totals[r].astype(jnp.bfloat16)
            mine[:, r * block : (r + 1) * block] = rows[:clen]
            sib[:, r * block : (r + 1) * block] = rows[clen:]


def project(context, weights):
    rows, local = context.shape
    pieces, row = [], 0
    for weight in weights:
        pieces.append((row // local, row % local))
        row += weight.shape[0]
    width = row // local * weights[0].shape[1]
    shape = jax.ShapeDtypeStruct((rows // 2, width), jnp.bfloat16)
    return pl.pallas_call(
        functools.partial(project_kernel, pieces),
        out_shape=[shape, shape],
        in_specs=[pl.BlockSpec(memory_space=pltpu.VMEM)] * (1 + len(weights)),
        out_specs=[pl.BlockSpec(memory_space=pltpu.VMEM)] * 2,
        compiler_params=VMEM,
        cost_estimate=small(),
        name="project",
    )(context, *weights)


def finish_kernel(parts, ids, counts, *refs):
    out_ref = refs[-1]
    chunks = (len(refs) - 1) // 3
    block = out_ref.shape[1] // parts
    live = jnp.where(ids[1] < counts[0], 1.0, 0.0)
    r = 0
    for chunk in range(chunks):
        mine, other, passed = refs[3 * chunk : 3 * chunk + 3]
        for start in range(0, mine.shape[1], block):
            columns = slice(start, start + block)
            total = mine[:, columns].astype(jnp.float32) + other[:, columns].astype(jnp.float32)
            total = total + passed[:, columns].astype(jnp.float32)
            target = pl.multiple_of(jnp.bitwise_xor(ids[0], r) * block, block)
            out_ref[:, pl.ds(target, block)] = (total * live).astype(jnp.bfloat16)
            r += 1


def finish(ids, counts, sums, parts, width):
    return pl.pallas_call(
        functools.partial(finish_kernel, parts),
        out_shape=jax.ShapeDtypeStruct((sums[0].shape[0], width), jnp.bfloat16),
        in_specs=[pl.BlockSpec(memory_space=pltpu.SMEM)] * 2
        + [pl.BlockSpec(memory_space=pltpu.VMEM)] * len(sums),
        out_specs=pl.BlockSpec(memory_space=pltpu.VMEM),
        compiler_params=VMEM,
        cost_estimate=small(),
        name="finish",
    )(ids, counts, *sums)


def shards(parts, devices, cand_states, enc_rows, w_query, w_key, w_value, w_out, tile_mask, counts):
    chips = devices // 2
    order = ring_order(chips)
    along = [
        (2 * order[i] + core, 2 * order[(i + 1) % chips] + core)
        for i in range(chips)
        for core in range(2)
    ]
    across = [(c, c ^ 1) for c in range(devices)]

    def to_next(value):
        return lax.ppermute(value, "cand", along)

    def to_sib(value):
        return lax.ppermute(value, "cand", across)

    def flip(value, r):
        return lax.ppermute(value, "prod", [(q, q ^ r) for q in range(parts)])

    ids = jnp.stack([lax.axis_index("prod"), lax.axis_index("cand")]).astype(jnp.int32)

    clen, width = cand_states.shape[2:]
    states = cand_states.reshape(clen, width)
    pairs = [(states, to_sib(states))]
    top = to_next(states[: clen // 2])

    half = w_query.shape[0] // 2
    if parts == 4:
        upper, lower = w_query[:half], w_query[half:]
        first = [flip(upper, 1), flip(lower, 2)]
    else:
        first = [flip(w_query, 1)]

    rows = enc_rows.shape[1]
    block = width // parts
    columns = column_blocks(ids, enc_rows.reshape(rows, width), parts)
    columns = [columns[0]] + [flip(columns[r], r) for r in range(1, parts)]
    tiles = tile_mask.shape[2]
    flags = tile_mask.reshape(1, tiles, 1).astype(jnp.bfloat16)
    flags = jnp.broadcast_to(flags, (FLAG_ROWS, tiles, block // tiles)).reshape(FLAG_ROWS, block)
    piece = jnp.concatenate(columns + [flags], axis=0)
    piece, top, first = lax.optimization_barrier((piece, top, first))
    gathered = lax.all_gather(piece, "cand", axis=0)

    states = jnp.concatenate([top, to_next(states[clen // 2 :])], axis=0)
    pairs.append((states, to_sib(states)))
    for _ in range(2, chips):
        states = to_next(states)
        pairs.append((states, to_sib(states)))
    if parts == 4:
        corner = [flip(first[0], 2), flip(first[1], 1)]
        query_parts = [w_query, first[0], flip(lower, 1), flip(upper, 2), first[1]] + corner
    else:
        query_parts = [w_query, first[0]] + [flip(w_query, r) for r in range(2, parts)]

    query_parts, w_out = lax.optimization_barrier((query_parts, w_out))
    out_parts = [w_out] + [flip(w_out, r) for r in range(1, parts if parts != 4 else 3)]
    if parts == 4:
        half = w_out.shape[0] // 2
        out_parts += [flip(out_parts[1][:half], 2), flip(out_parts[2][half:], 1)]
    out_chunks = [out_parts[: parts // 2], out_parts[parts // 2 :]]

    is_open, *sums = key_value(gathered, w_key, w_value, parts, rows, tiles)
    kv = sums[0]
    for r in range(1, parts):
        kv = kv + flip(sums[r], r).astype(jnp.float32)
    kv = kv.astype(jnp.bfloat16)

    passed = [None] * len(out_chunks)
    for step in list(range(1, chips)) + [0]:
        queries = query(ids, *pairs[step], query_parts, parts)
        context = attend(order, step, ids, queries, is_open, kv)
        last = []
        for chunk, weights in enumerate(out_chunks):
            mine, sib = project(context, weights)
            other = to_sib(sib)
            if step:
                total = mine.astype(jnp.float32) + other.astype(jnp.float32)
                if passed[chunk] is not None:
                    total = total + passed[chunk].astype(jnp.float32)
                passed[chunk] = to_next(total.astype(jnp.bfloat16))
            else:
                last += [mine, other, passed[chunk]]
    return finish(ids, counts, last, parts, width).reshape(cand_states.shape)


def solution(mesh):
    parts, devices = mesh.shape["prod"], mesh.shape["cand"]
    return jax.shard_map(
        functools.partial(shards, parts, devices),
        mesh=mesh,
        in_specs=(
            P("prod", "cand", None, None),
            P("prod", "cand", None),
            P("prod", "cand"),
            P("prod", "cand"),
            P("prod", "cand"),
            P("cand", "prod"),
            P("prod", "cand", None),
            P("prod"),
        ),
        out_specs=P("prod", "cand", None, None),
        check_vma=False,
    )
```

profile of v0, /device:TPU:0, one launch (start us, length us, event | category | flops | bytes accessed | tf_op | source)
XLA Modules:
  0.0 208.7 jit_solution(1689874965713693466)
XLA Ops:
  6.6 1.0 copy-done.17
  8.2 3.0 %collective-permute-start.1 = (bf16[32,1024]{1,0:T(8,128)(2,1)S(1)}, bf16[32,1024]{1,0:T(8,128)(2,1)S(1)}, u32[]{:S(2)}, u32[]{:S(2)}) collective-permute-start(bf16[32,1024]{1,0:T(8,128)(2,1)S(1)} %get-tuple-element.43), channel_id=1, source_target_pairs={{0,8},{8,0},{16,24},{24,16},{1,9},{9,1},{17,25},{25,17},{2,10},{10... | collective-permute-start | bytes 196616 | tf_op jit(solution)/shard_map/ppermute | solution.py:275
  11.2 1.5 collective-permute-start.2
  12.8 2.3 %slice_bitcast_fusion = (bf16[64,4096]{1,0:T(8,128)(2,1)}, bf16[64,4096]{1,0:T(8,128)(2,1)}) fusion(bf16[1,1,128,4096]{3,2,1,0:T(8,128)(2,1)} %param.8), kind=kLoop, calls=%fused_computation.7 | loop fusion | bytes 2097152 | tf_op jit(solution)/shard_map/slice | solution.py:302
  15.0 2.0 collective-permute-start.4
  17.1 1.0 fusion
  18.1 1.5 collective-permute-start.5
  19.7 1.6 collective-permute-start.6
  21.3 8.0 %collective-permute-done.4 = bf16[64,4096]{1,0:T(8,128)(2,1)S(1)} collective-permute-done((bf16[64,4096]{1,0:T(8,128)(2,1)}, bf16[64,4096]{1,0:T(8,128)(2,1)S(1)}, u32[]{:S(2)}, u32[]{:S(2)}) %collective-permute-start.4) | collective-permute-done | bytes 524320 | tf_op jit(solution)/shard_map/ppermute | solution.py:269
  29.4 1.5 collective-permute-done.5.refs_1_
  30.8 1.4 collective-permute-done.6.refs_4_
  32.3 2.6 %collective-permute-start.16 = (bf16[64,4096]{1,0:T(8,128)(2,1)}, bf16[64,4096]{1,0:T(8,128)(2,1)S(1)}, u32[]{:S(2)}, u32[]{:S(2)}) collective-permute-start(bf16[64,4096]{1,0:T(8,128)(2,1)} %get-tuple-element.79), channel_id=1, source_target_pairs={{0,2},{1,3},{2,6},{3,7},{6,4},{7,5},{4,0},{5,1},{8,10},{9,11},{10,... | collective-permute-start | bytes 1572872 | tf_op jit(solution)/shard_map/ppermute | solution.py:269
  35.4 1.5 collective-permute-start.8
  37.5 1.5 collective-permute-start.10
  39.0 0.8 constant_dynamic-update-slice_fusion.6
  39.8 12.4 %collective-permute-done.16 = bf16[64,4096]{1,0:T(8,128)(2,1)S(1)} collective-permute-done((bf16[64,4096]{1,0:T(8,128)(2,1)}, bf16[64,4096]{1,0:T(8,128)(2,1)S(1)}, u32[]{:S(2)}, u32[]{:S(2)}) %collective-permute-start.16) | collective-permute-done | bytes 524320 | tf_op jit(solution)/shard_map/ppermute | solution.py:269
  52.2 0.8 constant_dynamic-update-slice_fusion.5.mine
  53.0 0.8 copy-done.5
  53.8 1.9 collective-permute-start.17
  55.7 0.8 copy-done.7
  56.5 1.2 collective-permute-done.9.refs_5_
  57.7 0.8 copy-done.9
  58.5 0.8 copy-done.11
  59.3 1.5 collective-permute-start.14
  60.8 1.5 collective-permute-start.28
  62.3 7.1 %all-gather.3.cloned.1.call-done = bf16[1152,1024]{1,0:T(8,128)(2,1)} async-done(((bf16[144,1024]{1,0:T(8,128)(2,1)}), bf16[1152,1024]{1,0:T(8,128)(2,1)}) %all-gather.3.cloned.1.call-update) | async-done | bytes 2359312 | tf_op jit(solution)/shard_map/all_gather | solution.py:300
  69.4 1.8 copy-done.14
  71.2 1.2 copy-done.15
  72.4 1.2 copy-done.16
  73.7 2.3 %key_value.1 = (f32[8,256]{1,0:T(8,128)S(1)}, f32[256,1024]{1,0:T(8,128)S(1)}, bf16[256,1024]{1,0:T(8,128)(2,1)S(1)}, bf16[256,1024]{1,0:T(8,128)(2,1)S(1)}, bf16[256,1024]{1,0:T(8,128)(2,1)S(1)}) custom-call(bf16[8,144,1024]{2,1,0:T(8,128)(2,1)S(1)} %bitcast.17, bf16[1024,512]{1,0:T(8,128)(2,1)S(1)} %copy-done.15, bf16[1024,512]{1,0:T(8,128)(2,1)S(1)} %copy-done.16), custom_call_target="tpu_custom_call" | custom-call | flops 1 | bytes 1 | tf_op jit(solution)/shard_map/key_value/pallas_call | solution.py:76
  76.0 3.1 %collective-permute-start.13 = (bf16[256,1024]{1,0:T(8,128)(2,1)S(1)}, bf16[256,1024]{1,0:T(8,128)(2,1)S(1)}, u32[]{:S(2)}, u32[]{:S(2)}) collective-permute-start(bf16[256,1024]{1,0:T(8,128)(2,1)S(1)} %get-tuple-element.60), channel_id=1, source_target_pairs={{0,24},{8,16},{16,8},{24,0},{1,25},{9,17},{17,9},{25,1},{2,26},{10... | collective-permute-start | bytes 1572872 | tf_op jit(solution)/shard_map/ppermute | solution.py:275
  79.7 6.6 %collective-permute-done.17.mine = bf16[128,4096]{1,0:T(8,128)(2,1)} collective-permute-done((bf16[128,4096]{1,0:T(8,128)(2,1)}, bf16[128,4096]{1,0:T(8,128)(2,1)}, u32[]{:S(2)}, u32[]{:S(2)}) %collective-permute-start.17) | collective-permute-done | bytes 1048608 | tf_op jit(solution)/shard_map/ppermute | solution.py:269
  86.9 1.6 collective-permute-start.18
  88.5 7.9 %collective-permute-done.28.refs_0_ = bf16[512,1024]{1,0:T(8,128)(2,1)S(1)} collective-permute-done((bf16[512,1024]{1,0:T(8,128)(2,1)}, bf16[512,1024]{1,0:T(8,128)(2,1)S(1)}, u32[]{:S(2)}, u32[]{:S(2)}) %collective-permute-start.28) | collective-permute-done | bytes 1048608 | tf_op jit(solution)/shard_map/ppermute | solution.py:275
  96.4 3.3 %query.7.query_ref = bf16[256,512]{1,0:T(8,128)(2,1)S(1)} custom-call(s32[2]{0:T(128)S(1)} %pad_add_fusion.ids, bf16[128,4096]{1,0:T(8,128)(2,1)} %constant_dynamic-update-slice_fusion.5.mine, bf16[128,4096]{1,0:T(8,128)(2,1)} %collective-permute-done.23.sib, bf16[1024,512]{1,0:T(8,128)(2,1)S(1)} %copy-done, bf16[512,512]{1,0:T(8,128)(2,1)S(1)} %copy-done.2, ...), custom_call_target="tpu_custom_call" | custom-call | flops 1 | bytes 1 | tf_op jit(solution)/shard_map/query/pallas_call | solution.py:119
  99.8 2.6 %collective-permute-start.29 = (bf16[256,1024]{1,0:T(8,128)(2,1)S(1)}, bf16[256,1024]{1,0:T(8,128)(2,1)S(1)}, u32[]{:S(2)}, u32[]{:S(2)}) collective-permute-start(bf16[256,1024]{1,0:T(8,128)(2,1)S(1)} %slice.32), channel_id=1, source_target_pairs={{0,16},{8,24},{16,0},{24,8},{1,17},{9,25},{17,1},{25,9},{2,18},{10... | collective-permute-start | bytes 1572872 | tf_op jit(solution)/shard_map/ppermute | solution.py:275
  102.4 5.7 %collective-permute-done.12 = bf16[256,1024]{1,0:T(8,128)(2,1)S(1)} collective-permute-done((bf16[256,1024]{1,0:T(8,128)(2,1)S(1)}, bf16[256,1024]{1,0:T(8,128)(2,1)S(1)}, u32[]{:S(2)}, u32[]{:S(2)}) %collective-permute-start.12) | collective-permute-done | bytes 524320 | tf_op jit(solution)/shard_map/ppermute | solution.py:275
  108.1 2.0 collective-permute-start.30
  110.5 2.3 %attend.7.context_ref = bf16[256,512]{1,0:T(8,128)(2,1)S(1)} custom-call(s32[2]{0:T(128)S(1)} %pad_add_fusion.ids, bf16[256,512]{1,0:T(8,128)(2,1)S(1)} %query.7.query_ref, f32[8,256]{1,0:T(8,128)S(1)} %get-tuple-element.56.open_ref, bf16[256,1024]{1,0:T(8,128)(2,1)S(1)} %add_convert_fusion.6.kv_ref), custom_call_target="tpu_custom_call" | custom-call | flops 1 | bytes 1 | tf_op jit(solution)/shard_map/attend/pallas_call | solution.py:179
  112.7 1.9 project.11
  115.2 2.1 collective-permute-done.29.refs_1_
  118.8 2.9 %query.6.query_ref = bf16[256,512]{1,0:T(8,128)(2,1)S(1)} custom-call(s32[2]{0:T(128)S(1)} %pad_add_fusion.ids, bf16[128,4096]{1,0:T(8,128)(2,1)} %collective-permute-done.17.mine, bf16[128,4096]{1,0:T(8,128)(2,1)S(1)} %collective-permute-done.21.sib, bf16[1024,512]{1,0:T(8,128)(2,1)S(1)} %copy-done, bf16[512,512]{1,0:T(8,128)(2,1)S(1)} %copy-done.2, ...), custom_call_target="tpu_custom_call" | custom-call | flops 1 | bytes 1 | tf_op jit(solution)/shard_map/query/pallas_call | solution.py:119
  121.8 2.2 %attend.6.context_ref = bf16[256,512]{1,0:T(8,128)(2,1)S(1)} custom-call(s32[2]{0:T(128)S(1)} %pad_add_fusion.ids, bf16[256,512]{1,0:T(8,128)(2,1)S(1)} %query.6.query_ref, f32[8,256]{1,0:T(8,128)S(1)} %get-tuple-element.56.open_ref, bf16[256,1024]{1,0:T(8,128)(2,1)S(1)} %add_convert_fusion.6.kv_ref), custom_call_target="tpu_custom_call" | custom-call | flops 1 | bytes 1 | tf_op jit(solution)/shard_map/attend/pallas_call | solution.py:179
  124.0 1.9 project.10
  126.6 5.7 %collective-permute-start.25 = (bf16[128,2048]{1,0:T(8,128)(2,1)S(1)}, bf16[128,2048]{1,0:T(8,128)(2,1)S(1)}, u32[]{:S(2)}, u32[]{:S(2)}) collective-permute-start(bf16[128,2048]{1,0:T(8,128)(2,1)S(1)} %add_convert_fusion.5), channel_id=1, source_target_pairs={{0,2},{1,3},{2,6},{3,7},{6,4},{7,5},{4,0},{5,1},{8,10},{9,11},{10,... | collective-permute-start | bytes 1572872 | tf_op jit(solution)/shard_map/ppermute | solution.py:269
  132.4 0.7 project.14
  134.5 2.2 %query.5.query_ref = bf16[256,512]{1,0:T(8,128)(2,1)S(1)} custom-call(s32[2]{0:T(128)S(1)} %pad_add_fusion.ids, bf16[128,4096]{1,0:T(8,128)(2,1)S(1)} %collective-permute-done.18.mine, bf16[128,4096]{1,0:T(8,128)(2,1)S(1)} %collective-permute-done.19.sib, bf16[1024,512]{1,0:T(8,128)(2,1)S(1)} %copy-done, bf16[512,512]{1,0:T(8,128)(2,1)S(1)} %copy-done.2, ...), custom_call_target="tpu_custom_call" | custom-call | flops 1 | bytes 1 | tf_op jit(solution)/shard_map/query/pallas_call | solution.py:119
  136.7 2.3 %attend.5.context_ref = bf16[256,512]{1,0:T(8,128)(2,1)S(1)} custom-call(s32[2]{0:T(128)S(1)} %pad_add_fusion.ids, bf16[256,512]{1,0:T(8,128)(2,1)S(1)} %query.5.query_ref, f32[8,256]{1,0:T(8,128)S(1)} %get-tuple-element.56.open_ref, bf16[256,1024]{1,0:T(8,128)(2,1)S(1)} %add_convert_fusion.6.kv_ref), custom_call_target="tpu_custom_call" | custom-call | flops 1 | bytes 1 | tf_op jit(solution)/shard_map/attend/pallas_call | solution.py:179
  139.0 1.9 project.9
  140.9 0.7 project.13
  141.7 3.0 %collective-permute-done.25 = bf16[128,2048]{1,0:T(8,128)(2,1)S(1)} collective-permute-done((bf16[128,2048]{1,0:T(8,128)(2,1)S(1)}, bf16[128,2048]{1,0:T(8,128)(2,1)S(1)}, u32[]{:S(2)}, u32[]{:S(2)}) %collective-permute-start.25) | collective-permute-done | bytes 524320 | tf_op jit(solution)/shard_map/ppermute | solution.py:269
  144.9 2.5 %collective-permute-start.26 = (bf16[128,2048]{1,0:T(8,128)(2,1)S(1)}, bf16[128,2048]{1,0:T(8,128)(2,1)S(1)}, u32[]{:S(2)}, u32[]{:S(2)}) collective-permute-start(bf16[128,2048]{1,0:T(8,128)(2,1)S(1)} %add_convert_fusion.4), channel_id=1, source_target_pairs={{0,2},{1,3},{2,6},{3,7},{6,4},{7,5},{4,0},{5,1},{8,10},{9,11},{10,... | collective-permute-start | bytes 1572872 | tf_op jit(solution)/shard_map/ppermute | solution.py:269
  147.5 8.4 %collective-permute-done.35 = bf16[128,2048]{1,0:T(8,128)(2,1)S(1)} collective-permute-done((bf16[128,2048]{1,0:T(8,128)(2,1)S(1)}, bf16[128,2048]{1,0:T(8,128)(2,1)S(1)}, u32[]{:S(2)}, u32[]{:S(2)}) %collective-permute-start.35) | collective-permute-done | bytes 524320 | tf_op jit(solution)/shard_map/ppermute | solution.py:269
  156.2 2.5 %collective-permute-start.36 = (bf16[128,2048]{1,0:T(8,128)(2,1)S(1)}, bf16[128,2048]{1,0:T(8,128)(2,1)S(1)}, u32[]{:S(2)}, u32[]{:S(2)}) collective-permute-start(bf16[128,2048]{1,0:T(8,128)(2,1)S(1)} %add_convert_fusion.1), channel_id=1, source_target_pairs={{0,2},{1,3},{2,6},{3,7},{6,4},{7,5},{4,0},{5,1},{8,10},{9,11},{10,... | collective-permute-start | bytes 1572872 | tf_op jit(solution)/shard_map/ppermute | solution.py:269
  158.7 2.2 %query.4.query_ref = bf16[256,512]{1,0:T(8,128)(2,1)S(1)} custom-call(s32[2]{0:T(128)S(1)} %pad_add_fusion.ids, bf16[128,4096]{1,0:T(8,128)(2,1)S(1)} %bitcast.16, bf16[128,4096]{1,0:T(8,128)(2,1)S(1)} %collective-permute-done.sib, bf16[1024,512]{1,0:T(8,128)(2,1)S(1)} %copy-done, bf16[512,512]{1,0:T(8,128)(2,1)S(1)} %copy-done.2, ...), custom_call_target="tpu_custom_call" | custom-call | flops 1 | bytes 1 | tf_op jit(solution)/shard_map/query/pallas_call | solution.py:119
  160.9 2.3 %attend.4.context_ref = bf16[256,512]{1,0:T(8,128)(2,1)S(1)} custom-call(s32[2]{0:T(128)S(1)} %pad_add_fusion.ids, bf16[256,512]{1,0:T(8,128)(2,1)S(1)} %query.4.query_ref, f32[8,256]{1,0:T(8,128)S(1)} %get-tuple-element.56.open_ref, bf16[256,1024]{1,0:T(8,128)(2,1)S(1)} %add_convert_fusion.6.kv_ref), custom_call_target="tpu_custom_call" | custom-call | flops 1 | bytes 1 | tf_op jit(solution)/shard_map/attend/pallas_call | solution.py:179
  163.2 1.9 project.8
  165.2 0.7 project.12
  167.4 2.5 %collective-permute-start.27 = (bf16[128,2048]{1,0:T(8,128)(2,1)S(1)}, bf16[128,2048]{1,0:T(8,128)(2,1)S(1)}, u32[]{:S(2)}, u32[]{:S(2)}) collective-permute-start(bf16[128,2048]{1,0:T(8,128)(2,1)S(1)} %add_convert_fusion.3), channel_id=1, source_target_pairs={{0,2},{1,3},{2,6},{3,7},{6,4},{7,5},{4,0},{5,1},{8,10},{9,11},{10,... | collective-permute-start | bytes 1572872 | tf_op jit(solution)/shard_map/ppermute | solution.py:269
  169.9 8.4 %collective-permute-done.36 = bf16[128,2048]{1,0:T(8,128)(2,1)S(1)} collective-permute-done((bf16[128,2048]{1,0:T(8,128)(2,1)S(1)}, bf16[128,2048]{1,0:T(8,128)(2,1)S(1)}, u32[]{:S(2)}, u32[]{:S(2)}) %collective-permute-start.36) | collective-permute-done | bytes 524320 | tf_op jit(solution)/shard_map/ppermute | solution.py:269
  178.6 2.5 %collective-permute-start.37 = (bf16[128,2048]{1,0:T(8,128)(2,1)S(1)}, bf16[128,2048]{1,0:T(8,128)(2,1)S(1)}, u32[]{:S(2)}, u32[]{:S(2)}) collective-permute-start(bf16[128,2048]{1,0:T(8,128)(2,1)S(1)} %add_convert_fusion), channel_id=1, source_target_pairs={{0,2},{1,3},{2,6},{3,7},{6,4},{7,5},{4,0},{5,1},{8,10},{9,11},{10,... | collective-permute-start | bytes 1572872 | tf_op jit(solution)/shard_map/ppermute | solution.py:269
  181.8 7.8 %collective-permute-done.27.refs_2_ = bf16[128,2048]{1,0:T(8,128)(2,1)S(1)} collective-permute-done((bf16[128,2048]{1,0:T(8,128)(2,1)S(1)}, bf16[128,2048]{1,0:T(8,128)(2,1)S(1)}, u32[]{:S(2)}, u32[]{:S(2)}) %collective-permute-start.27) | collective-permute-done | bytes 524320 | tf_op jit(solution)/shard_map/ppermute | solution.py:269
  189.6 10.3 %collective-permute-done.37.refs_5_ = bf16[128,2048]{1,0:T(8,128)(2,1)S(1)} collective-permute-done((bf16[128,2048]{1,0:T(8,128)(2,1)S(1)}, bf16[128,2048]{1,0:T(8,128)(2,1)S(1)}, u32[]{:S(2)}, u32[]{:S(2)}) %collective-permute-start.37) | collective-permute-done | bytes 524320 | tf_op jit(solution)/shard_map/ppermute | solution.py:269
  199.9 2.0 finish.1
  (96 shorter events, 9.8 us)
Async XLA Ops:
  6.5 10.5 %copy-start = (bf16[1024,512]{1,0:T(8,128)(2,1)S(1)}, bf16[1024,512]{1,0:T(8,128)(2,1)}, u32[]{:S(2)}) copy-start(bf16[1024,512]{1,0:T(8,128)(2,1)} %refs_0_.6) | copy-start | bytes 3145732
  6.5 62.8 %all-gather.3.cloned.1.call-start = ((), (), s32[]{:S(2)}) async-start(), calls=%async_computation | async-start | bytes 2654208 | tf_op jit(solution)/shard_map/all_gather | solution.py:300
  6.6 1.0 copy-start.17
  7.6 11.9 %copy-start.19 = (s32[1,1,2]{2,1,0:T(1,128)S(1)}, s32[1,1,2]{2,1,0:T(1,128)}, u32[]{:S(2)}) copy-start(s32[1,1,2]{2,1,0:T(1,128)} %param.14) | copy-start | bytes 28
  8.2 11.5 %collective-permute-start.1 = (bf16[32,1024]{1,0:T(8,128)(2,1)S(1)}, bf16[32,1024]{1,0:T(8,128)(2,1)S(1)}, u32[]{:S(2)}, u32[]{:S(2)}) collective-permute-start(bf16[32,1024]{1,0:T(8,128)(2,1)S(1)} %get-tuple-element.43), channel_id=1, source_target_pairs={{0,8},{8,0},{16,24},{24,16},{1,9},{9,1},{17,25},{25,17},{2,10},{10... | collective-permute-start | bytes 196616 | tf_op jit(solution)/shard_map/ppermute | solution.py:275
  11.2 10.1 %collective-permute-start.2 = (bf16[32,1024]{1,0:T(8,128)(2,1)S(1)}, bf16[32,1024]{1,0:T(8,128)(2,1)S(1)}, u32[]{:S(2)}, u32[]{:S(2)}) collective-permute-start(bf16[32,1024]{1,0:T(8,128)(2,1)S(1)} %get-tuple-element.44), channel_id=1, source_target_pairs={{0,16},{8,24},{16,0},{24,8},{1,17},{9,25},{17,1},{25,9},{2,18},{10... | collective-permute-start | bytes 196616 | tf_op jit(solution)/shard_map/ppermute | solution.py:275
  12.7 8.6 %collective-permute-start.3 = (bf16[32,1024]{1,0:T(8,128)(2,1)S(1)}, bf16[32,1024]{1,0:T(8,128)(2,1)S(1)}, u32[]{:S(2)}, u32[]{:S(2)}) collective-permute-start(bf16[32,1024]{1,0:T(8,128)(2,1)S(1)} %get-tuple-element.45), channel_id=1, source_target_pairs={{0,24},{8,16},{16,8},{24,0},{1,25},{9,17},{17,9},{25,1},{2,26},{10... | collective-permute-start | bytes 196616 | tf_op jit(solution)/shard_map/ppermute | solution.py:275
  15.0 14.3 %collective-permute-start.4 = (bf16[64,4096]{1,0:T(8,128)(2,1)}, bf16[64,4096]{1,0:T(8,128)(2,1)S(1)}, u32[]{:S(2)}, u32[]{:S(2)}) collective-permute-start(bf16[64,4096]{1,0:T(8,128)(2,1)} %get-tuple-element.80), channel_id=1, source_target_pairs={{0,2},{1,3},{2,6},{3,7},{6,4},{7,5},{4,0},{5,1},{8,10},{9,11},{10,... | collective-permute-start | bytes 1572872 | tf_op jit(solution)/shard_map/ppermute | solution.py:269
  18.1 12.8 %collective-permute-start.5 = (bf16[512,512]{1,0:T(8,128)(2,1)}, bf16[512,512]{1,0:T(8,128)(2,1)S(1)}, u32[]{:S(2)}, u32[]{:S(2)}) collective-permute-start(bf16[512,512]{1,0:T(8,128)(2,1)} %get-tuple-element.82), channel_id=1, source_target_pairs={{0,8},{8,0},{16,24},{24,16},{1,9},{9,1},{17,25},{25,17},{2,10},{10... | collective-permute-start | bytes 1572872 | tf_op jit(solution)/shard_map/ppermute | solution.py:275
  19.7 12.5 %collective-permute-start.6 = (bf16[512,512]{1,0:T(8,128)(2,1)}, bf16[512,512]{1,0:T(8,128)(2,1)S(1)}, u32[]{:S(2)}, u32[]{:S(2)}) collective-permute-start(bf16[512,512]{1,0:T(8,128)(2,1)} %get-tuple-element.81), channel_id=1, source_target_pairs={{0,16},{8,24},{16,0},{24,8},{1,17},{9,25},{17,1},{25,9},{2,18},{10... | collective-permute-start | bytes 1572872 | tf_op jit(solution)/shard_map/ppermute | solution.py:275
  21.3 10.9 %copy-start.18 = (bf16[144,1024]{1,0:T(8,128)(2,1)}, bf16[144,1024]{1,0:T(8,128)(2,1)S(1)}, u32[]{:S(2)}) copy-start(bf16[144,1024]{1,0:T(8,128)(2,1)S(1)} %constant_dynamic-update-slice_fusion) | copy-start | bytes 884740
  30.8 27.6 %copy-start.1 = (bf16[512,512]{1,0:T(8,128)(2,1)}, bf16[512,512]{1,0:T(8,128)(2,1)S(1)}, u32[]{:S(2)}) copy-start(bf16[512,512]{1,0:T(8,128)(2,1)S(1)} %collective-permute-done.5.refs_1_) | copy-start | bytes 1572868
  32.2 26.2 %copy-start.3 = (bf16[512,512]{1,0:T(8,128)(2,1)}, bf16[512,512]{1,0:T(8,128)(2,1)S(1)}, u32[]{:S(2)}) copy-start(bf16[512,512]{1,0:T(8,128)(2,1)S(1)} %collective-permute-done.6.refs_4_) | copy-start | bytes 1572868
  32.3 19.9 %collective-permute-start.16 = (bf16[64,4096]{1,0:T(8,128)(2,1)}, bf16[64,4096]{1,0:T(8,128)(2,1)S(1)}, u32[]{:S(2)}, u32[]{:S(2)}) collective-permute-start(bf16[64,4096]{1,0:T(8,128)(2,1)} %get-tuple-element.79), channel_id=1, source_target_pairs={{0,2},{1,3},{2,6},{3,7},{6,4},{7,5},{4,0},{5,1},{8,10},{9,11},{10,... | collective-permute-start | bytes 1572872 | tf_op jit(solution)/shard_map/ppermute | solution.py:269
  34.9 18.1 %collective-permute-start.7 = (bf16[512,512]{1,0:T(8,128)(2,1)}, bf16[512,512]{1,0:T(8,128)(2,1)S(1)}, u32[]{:S(2)}, u32[]{:S(2)}) collective-permute-start(bf16[512,512]{1,0:T(8,128)(2,1)} %get-tuple-element.81), channel_id=1, source_target_pairs={{0,8},{8,0},{16,24},{24,16},{1,9},{9,1},{17,25},{25,17},{2,10},{10... | collective-permute-start | bytes 1572872 | tf_op jit(solution)/shard_map/ppermute | solution.py:275
  35.4 20.2 %collective-permute-start.8 = (bf16[512,512]{1,0:T(8,128)(2,1)}, bf16[512,512]{1,0:T(8,128)(2,1)S(1)}, u32[]{:S(2)}, u32[]{:S(2)}) collective-permute-start(bf16[512,512]{1,0:T(8,128)(2,1)} %get-tuple-element.82), channel_id=1, source_target_pairs={{0,16},{8,24},{16,0},{24,8},{1,17},{9,25},{17,1},{25,9},{2,18},{10... | collective-permute-start | bytes 1572872 | tf_op jit(solution)/shard_map/ppermute | solution.py:275
  37.0 20.7 %collective-permute-start.9 = (bf16[512,512]{1,0:T(8,128)(2,1)S(1)}, bf16[512,512]{1,0:T(8,128)(2,1)S(1)}, u32[]{:S(2)}, u32[]{:S(2)}) collective-permute-start(bf16[512,512]{1,0:T(8,128)(2,1)S(1)} %collective-permute-done.5.refs_1_), channel_id=1, source_target_pairs={{0,16},{8,24},{16,0},{24,8},{1,17},{9,25},{17,1},{25,9},{2,18},{10... | collective-permute-start | bytes 1572872 | tf_op jit(solution)/shard_map/ppermute | solution.py:275
  37.5 21.0 %collective-permute-start.10 = (bf16[512,512]{1,0:T(8,128)(2,1)S(1)}, bf16[512,512]{1,0:T(8,128)(2,1)S(1)}, u32[]{:S(2)}, u32[]{:S(2)}) collective-permute-start(bf16[512,512]{1,0:T(8,128)(2,1)S(1)} %collective-permute-done.6.refs_4_), channel_id=1, source_target_pairs={{0,8},{8,0},{16,24},{24,16},{1,9},{9,1},{17,25},{25,17},{2,10},{10... | collective-permute-start | bytes 1572872 | tf_op jit(solution)/shard_map/ppermute | solution.py:275
  53.0 26.2 %collective-permute-start.23 = (bf16[128,4096]{1,0:T(8,128)(2,1)}, bf16[128,4096]{1,0:T(8,128)(2,1)}, u32[]{:S(2)}, u32[]{:S(2)}) collective-permute-start(bf16[128,4096]{1,0:T(8,128)(2,1)} %constant_dynamic-update-slice_fusion.5.mine), channel_id=1, source_target_pairs={{0,1},{1,0},{2,3},{3,2},{4,5},{5,4},{6,7},{7,6},{8,9},{9,8},{10,11... | collective-permute-start | bytes 3145736 | tf_op jit(solution)/shard_map/ppermute | solution.py:272
  53.0 0.8 copy-start.5
  53.8 32.6 %collective-permute-start.17 = (bf16[128,4096]{1,0:T(8,128)(2,1)}, bf16[128,4096]{1,0:T(8,128)(2,1)}, u32[]{:S(2)}, u32[]{:S(2)}) collective-permute-start(bf16[128,4096]{1,0:T(8,128)(2,1)} %constant_dynamic-update-slice_fusion.5.mine), channel_id=1, source_target_pairs={{0,2},{1,3},{2,6},{3,7},{6,4},{7,5},{4,0},{5,1},{8,10},{9,11},{10,... | collective-permute-start | bytes 3145736 | tf_op jit(solution)/shard_map/ppermute | solution.py:269
  55.7 0.8 copy-start.7
  57.7 0.8 copy-start.9
  58.5 0.8 copy-start.11
  59.3 27.6 %collective-permute-start.14 = (bf16[512,1024]{1,0:T(8,128)(2,1)}, bf16[512,1024]{1,0:T(8,128)(2,1)S(1)}, u32[]{:S(2)}, u32[]{:S(2)}) collective-permute-start(bf16[512,1024]{1,0:T(8,128)(2,1)} %refs_0_.7), channel_id=1, source_target_pairs={{0,8},{8,0},{16,24},{24,16},{1,9},{9,1},{17,25},{25,17},{2,10},{10... | collective-permute-start | bytes 3145736 | tf_op jit(solution)/shard_map/ppermute | solution.py:275
  60.8 35.6 %collective-permute-start.28 = (bf16[512,1024]{1,0:T(8,128)(2,1)}, bf16[512,1024]{1,0:T(8,128)(2,1)S(1)}, u32[]{:S(2)}, u32[]{:S(2)}) collective-permute-start(bf16[512,1024]{1,0:T(8,128)(2,1)} %refs_0_.7), channel_id=1, source_target_pairs={{0,16},{8,24},{16,0},{24,8},{1,17},{9,25},{17,1},{25,9},{2,18},{10... | collective-permute-start | bytes 3145736 | tf_op jit(solution)/shard_map/ppermute | solution.py:275
  69.4 27.0 %copy-start.2 = (bf16[512,512]{1,0:T(8,128)(2,1)S(1)}, bf16[512,512]{1,0:T(8,128)(2,1)}, u32[]{:S(2)}) copy-start(bf16[512,512]{1,0:T(8,128)(2,1)} %copy-done.1) | copy-start | bytes 1572868
  69.4 27.0 %copy-start.4 = (bf16[512,512]{1,0:T(8,128)(2,1)S(1)}, bf16[512,512]{1,0:T(8,128)(2,1)}, u32[]{:S(2)}) copy-start(bf16[512,512]{1,0:T(8,128)(2,1)} %copy-done.3) | copy-start | bytes 1572868
  69.4 27.0 %copy-start.6 = (bf16[512,512]{1,0:T(8,128)(2,1)S(1)}, bf16[512,512]{1,0:T(8,128)(2,1)}, u32[]{:S(2)}) copy-start(bf16[512,512]{1,0:T(8,128)(2,1)} %copy-done.5) | copy-start | bytes 1572868
  69.4 27.0 %copy-start.8 = (bf16[512,512]{1,0:T(8,128)(2,1)S(1)}, bf16[512,512]{1,0:T(8,128)(2,1)}, u32[]{:S(2)}) copy-start(bf16[512,512]{1,0:T(8,128)(2,1)} %copy-done.7) | copy-start | bytes 1572868
  69.4 27.1 %copy-start.10 = (bf16[512,512]{1,0:T(8,128)(2,1)S(1)}, bf16[512,512]{1,0:T(8,128)(2,1)}, u32[]{:S(2)}) copy-start(bf16[512,512]{1,0:T(8,128)(2,1)} %copy-done.9) | copy-start | bytes 1572868
  69.4 27.1 %copy-start.12 = (bf16[512,512]{1,0:T(8,128)(2,1)S(1)}, bf16[512,512]{1,0:T(8,128)(2,1)}, u32[]{:S(2)}) copy-start(bf16[512,512]{1,0:T(8,128)(2,1)} %copy-done.11) | copy-start | bytes 1572868
  69.4 1.8 copy-start.14
  71.2 1.2 copy-start.15
  72.4 1.2 copy-start.16
  76.0 23.8 %collective-permute-start.13 = (bf16[256,1024]{1,0:T(8,128)(2,1)S(1)}, bf16[256,1024]{1,0:T(8,128)(2,1)S(1)}, u32[]{:S(2)}, u32[]{:S(2)}) collective-permute-start(bf16[256,1024]{1,0:T(8,128)(2,1)S(1)} %get-tuple-element.60), channel_id=1, source_target_pairs={{0,24},{8,16},{16,8},{24,0},{1,25},{9,17},{17,9},{25,1},{2,26},{10... | collective-permute-start | bytes 1572872 | tf_op jit(solution)/shard_map/ppermute | solution.py:275
  79.1 29.0 %collective-permute-start.12 = (bf16[256,1024]{1,0:T(8,128)(2,1)S(1)}, bf16[256,1024]{1,0:T(8,128)(2,1)S(1)}, u32[]{:S(2)}, u32[]{:S(2)}) collective-permute-start(bf16[256,1024]{1,0:T(8,128)(2,1)S(1)} %get-tuple-element.59), channel_id=1, source_target_pairs={{0,16},{8,24},{16,0},{24,8},{1,17},{9,25},{17,1},{25,9},{2,18},{10... | collective-permute-start | bytes 1572872 | tf_op jit(solution)/shard_map/ppermute | solution.py:275
  86.4 23.7 %collective-permute-start.11 = (bf16[256,1024]{1,0:T(8,128)(2,1)S(1)}, bf16[256,1024]{1,0:T(8,128)(2,1)S(1)}, u32[]{:S(2)}, u32[]{:S(2)}) collective-permute-start(bf16[256,1024]{1,0:T(8,128)(2,1)S(1)} %get-tuple-element.58), channel_id=1, source_target_pairs={{0,8},{8,0},{16,24},{24,16},{1,9},{9,1},{17,25},{25,17},{2,10},{10... | collective-permute-start | bytes 1572872 | tf_op jit(solution)/shard_map/ppermute | solution.py:275
  86.9 27.9 %collective-permute-start.18 = (bf16[128,4096]{1,0:T(8,128)(2,1)}, bf16[128,4096]{1,0:T(8,128)(2,1)S(1)}, u32[]{:S(2)}, u32[]{:S(2)}) collective-permute-start(bf16[128,4096]{1,0:T(8,128)(2,1)} %collective-permute-done.17.mine), channel_id=1, source_target_pairs={{0,2},{1,3},{2,6},{3,7},{6,4},{7,5},{4,0},{5,1},{8,10},{9,11},{10,... | collective-permute-start | bytes 3145736 | tf_op jit(solution)/shard_map/ppermute | solution.py:269
  96.4 22.4 %collective-permute-start.21 = (bf16[128,4096]{1,0:T(8,128)(2,1)}, bf16[128,4096]{1,0:T(8,128)(2,1)S(1)}, u32[]{:S(2)}, u32[]{:S(2)}) collective-permute-start(bf16[128,4096]{1,0:T(8,128)(2,1)} %collective-permute-done.17.mine), channel_id=1, source_target_pairs={{0,1},{1,0},{2,3},{3,2},{4,5},{5,4},{6,7},{7,6},{8,9},{9,8},{10,11... | collective-permute-start | bytes 3145736 | tf_op jit(solution)/shard_map/ppermute | solution.py:272
  99.8 17.5 %collective-permute-start.29 = (bf16[256,1024]{1,0:T(8,128)(2,1)S(1)}, bf16[256,1024]{1,0:T(8,128)(2,1)S(1)}, u32[]{:S(2)}, u32[]{:S(2)}) collective-permute-start(bf16[256,1024]{1,0:T(8,128)(2,1)S(1)} %slice.32), channel_id=1, source_target_pairs={{0,16},{8,24},{16,0},{24,8},{1,17},{9,25},{17,1},{25,9},{2,18},{10... | collective-permute-start | bytes 1572872 | tf_op jit(solution)/shard_map/ppermute | solution.py:275
  108.1 9.9 %collective-permute-start.30 = (bf16[256,1024]{1,0:T(8,128)(2,1)S(1)}, bf16[256,1024]{1,0:T(8,128)(2,1)S(1)}, u32[]{:S(2)}, u32[]{:S(2)}) collective-permute-start(bf16[256,1024]{1,0:T(8,128)(2,1)S(1)} %slice.33), channel_id=1, source_target_pairs={{0,8},{8,0},{16,24},{24,16},{1,9},{9,1},{17,25},{25,17},{2,10},{10... | collective-permute-start | bytes 1572872 | tf_op jit(solution)/shard_map/ppermute | solution.py:275
  114.7 11.8 %collective-permute-start.24 = (bf16[128,2048]{1,0:T(8,128)(2,1)S(1)}, bf16[128,2048]{1,0:T(8,128)(2,1)S(1)}, u32[]{:S(2)}, u32[]{:S(2)}) collective-permute-start(bf16[128,2048]{1,0:T(8,128)(2,1)S(1)} %get-tuple-element.70), channel_id=1, source_target_pairs={{0,1},{1,0},{2,3},{3,2},{4,5},{5,4},{6,7},{7,6},{8,9},{9,8},{10,11... | collective-permute-start | bytes 1572872 | tf_op jit(solution)/shard_map/ppermute | solution.py:272
  114.8 19.1 %collective-permute-start.19 = (bf16[128,4096]{1,0:T(8,128)(2,1)S(1)}, bf16[128,4096]{1,0:T(8,128)(2,1)S(1)}, u32[]{:S(2)}, u32[]{:S(2)}) collective-permute-start(bf16[128,4096]{1,0:T(8,128)(2,1)S(1)} %collective-permute-done.18.mine), channel_id=1, source_target_pairs={{0,1},{1,0},{2,3},{3,2},{4,5},{5,4},{6,7},{7,6},{8,9},{9,8},{10,11... | collective-permute-start | bytes 3145736 | tf_op jit(solution)/shard_map/ppermute | solution.py:272
  118.7 14.4 %collective-permute-start.34 = (bf16[128,2048]{1,0:T(8,128)(2,1)S(1)}, bf16[128,2048]{1,0:T(8,128)(2,1)S(1)}, u32[]{:S(2)}, u32[]{:S(2)}) collective-permute-start(bf16[128,2048]{1,0:T(8,128)(2,1)S(1)} %get-tuple-element.78), channel_id=1, source_target_pairs={{0,1},{1,0},{2,3},{3,2},{4,5},{5,4},{6,7},{7,6},{8,9},{9,8},{10,11... | collective-permute-start | bytes 1572872 | tf_op jit(solution)/shard_map/ppermute | solution.py:272
  121.7 10.6 %copy-start.13 = (bf16[1,1,128,4096]{3,2,1,0:T(8,128)(2,1)S(1)}, bf16[1,1,128,4096]{3,2,1,0:T(8,128)(2,1)}, u32[]{:S(2)}) copy-start(bf16[1,1,128,4096]{3,2,1,0:T(8,128)(2,1)} %param.8) | copy-start | bytes 3145732
  126.0 15.7 %collective-permute-start.22 = (bf16[128,2048]{1,0:T(8,128)(2,1)S(1)}, bf16[128,2048]{1,0:T(8,128)(2,1)S(1)}, u32[]{:S(2)}, u32[]{:S(2)}) collective-permute-start(bf16[128,2048]{1,0:T(8,128)(2,1)S(1)} %get-tuple-element.68), channel_id=1, source_target_pairs={{0,1},{1,0},{2,3},{3,2},{4,5},{5,4},{6,7},{7,6},{8,9},{9,8},{10,11... | collective-permute-start | bytes 1572872 | tf_op jit(solution)/shard_map/ppermute | solution.py:272
  126.6 18.0 %collective-permute-start.25 = (bf16[128,2048]{1,0:T(8,128)(2,1)S(1)}, bf16[128,2048]{1,0:T(8,128)(2,1)S(1)}, u32[]{:S(2)}, u32[]{:S(2)}) collective-permute-start(bf16[128,2048]{1,0:T(8,128)(2,1)S(1)} %add_convert_fusion.5), channel_id=1, source_target_pairs={{0,2},{1,3},{2,6},{3,7},{6,4},{7,5},{4,0},{5,1},{8,10},{9,11},{10,... | collective-permute-start | bytes 1572872 | tf_op jit(solution)/shard_map/ppermute | solution.py:269
  132.4 26.3 %collective-permute-start = (bf16[128,4096]{1,0:T(8,128)(2,1)S(1)}, bf16[128,4096]{1,0:T(8,128)(2,1)S(1)}, u32[]{:S(2)}, u32[]{:S(2)}) collective-permute-start(bf16[128,4096]{1,0:T(8,128)(2,1)S(1)} %bitcast.15), channel_id=1, source_target_pairs={{0,1},{1,0},{2,3},{3,2},{4,5},{5,4},{6,7},{7,6},{8,9},{9,8},{10,11... | collective-permute-start | bytes 3145736 | tf_op jit(solution)/shard_map/ppermute | solution.py:272
  133.1 14.3 %collective-permute-start.33 = (bf16[128,2048]{1,0:T(8,128)(2,1)S(1)}, bf16[128,2048]{1,0:T(8,128)(2,1)S(1)}, u32[]{:S(2)}, u32[]{:S(2)}) collective-permute-start(bf16[128,2048]{1,0:T(8,128)(2,1)S(1)} %get-tuple-element.76), channel_id=1, source_target_pairs={{0,1},{1,0},{2,3},{3,2},{4,5},{5,4},{6,7},{7,6},{8,9},{9,8},{10,11... | collective-permute-start | bytes 1572872 | tf_op jit(solution)/shard_map/ppermute | solution.py:272
  133.8 22.1 %collective-permute-start.35 = (bf16[128,2048]{1,0:T(8,128)(2,1)S(1)}, bf16[128,2048]{1,0:T(8,128)(2,1)S(1)}, u32[]{:S(2)}, u32[]{:S(2)}) collective-permute-start(bf16[128,2048]{1,0:T(8,128)(2,1)S(1)} %add_convert_fusion.2), channel_id=1, source_target_pairs={{0,2},{1,3},{2,6},{3,7},{6,4},{7,5},{4,0},{5,1},{8,10},{9,11},{10,... | collective-permute-start | bytes 1572872 | tf_op jit(solution)/shard_map/ppermute | solution.py:269
  141.6 24.3 %collective-permute-start.20 = (bf16[128,2048]{1,0:T(8,128)(2,1)S(1)}, bf16[128,2048]{1,0:T(8,128)(2,1)S(1)}, u32[]{:S(2)}, u32[]{:S(2)}) collective-permute-start(bf16[128,2048]{1,0:T(8,128)(2,1)S(1)} %get-tuple-element.66), channel_id=1, source_target_pairs={{0,1},{1,0},{2,3},{3,2},{4,5},{5,4},{6,7},{7,6},{8,9},{9,8},{10,11... | collective-permute-start | bytes 1572872 | tf_op jit(solution)/shard_map/ppermute | solution.py:272
  144.9 22.2 %collective-permute-start.26 = (bf16[128,2048]{1,0:T(8,128)(2,1)S(1)}, bf16[128,2048]{1,0:T(8,128)(2,1)S(1)}, u32[]{:S(2)}, u32[]{:S(2)}) collective-permute-start(bf16[128,2048]{1,0:T(8,128)(2,1)S(1)} %add_convert_fusion.4), channel_id=1, source_target_pairs={{0,2},{1,3},{2,6},{3,7},{6,4},{7,5},{4,0},{5,1},{8,10},{9,11},{10,... | collective-permute-start | bytes 1572872 | tf_op jit(solution)/shard_map/ppermute | solution.py:269
  147.5 22.5 %collective-permute-start.32 = (bf16[128,2048]{1,0:T(8,128)(2,1)S(1)}, bf16[128,2048]{1,0:T(8,128)(2,1)S(1)}, u32[]{:S(2)}, u32[]{:S(2)}) collective-permute-start(bf16[128,2048]{1,0:T(8,128)(2,1)S(1)} %get-tuple-element.74), channel_id=1, source_target_pairs={{0,1},{1,0},{2,3},{3,2},{4,5},{5,4},{6,7},{7,6},{8,9},{9,8},{10,11... | collective-permute-start | bytes 1572872 | tf_op jit(solution)/shard_map/ppermute | solution.py:272
  156.2 22.2 %collective-permute-start.36 = (bf16[128,2048]{1,0:T(8,128)(2,1)S(1)}, bf16[128,2048]{1,0:T(8,128)(2,1)S(1)}, u32[]{:S(2)}, u32[]{:S(2)}) collective-permute-start(bf16[128,2048]{1,0:T(8,128)(2,1)S(1)} %add_convert_fusion.1), channel_id=1, source_target_pairs={{0,2},{1,3},{2,6},{3,7},{6,4},{7,5},{4,0},{5,1},{8,10},{9,11},{10,... | collective-permute-start | bytes 1572872 | tf_op jit(solution)/shard_map/ppermute | solution.py:269
  165.1 16.7 %collective-permute-start.15 = (bf16[128,2048]{1,0:T(8,128)(2,1)S(1)}, bf16[128,2048]{1,0:T(8,128)(2,1)S(1)}, u32[]{:S(2)}, u32[]{:S(2)}) collective-permute-start(bf16[128,2048]{1,0:T(8,128)(2,1)S(1)} %get-tuple-element.63), channel_id=1, source_target_pairs={{0,1},{1,0},{2,3},{3,2},{4,5},{5,4},{6,7},{7,6},{8,9},{9,8},{10,11... | collective-permute-start | bytes 1572872 | tf_op jit(solution)/shard_map/ppermute | solution.py:272
  166.0 15.9 %collective-permute-start.31 = (bf16[128,2048]{1,0:T(8,128)(2,1)S(1)}, bf16[128,2048]{1,0:T(8,128)(2,1)S(1)}, u32[]{:S(2)}, u32[]{:S(2)}) collective-permute-start(bf16[128,2048]{1,0:T(8,128)(2,1)S(1)} %get-tuple-element.72), channel_id=1, source_target_pairs={{0,1},{1,0},{2,3},{3,2},{4,5},{5,4},{6,7},{7,6},{8,9},{9,8},{10,11... | collective-permute-start | bytes 1572872 | tf_op jit(solution)/shard_map/ppermute | solution.py:272
  167.4 22.2 %collective-permute-start.27 = (bf16[128,2048]{1,0:T(8,128)(2,1)S(1)}, bf16[128,2048]{1,0:T(8,128)(2,1)S(1)}, u32[]{:S(2)}, u32[]{:S(2)}) collective-permute-start(bf16[128,2048]{1,0:T(8,128)(2,1)S(1)} %add_convert_fusion.3), channel_id=1, source_target_pairs={{0,2},{1,3},{2,6},{3,7},{6,4},{7,5},{4,0},{5,1},{8,10},{9,11},{10,... | collective-permute-start | bytes 1572872 | tf_op jit(solution)/shard_map/ppermute | solution.py:269
  178.6 21.3 %collective-permute-start.37 = (bf16[128,2048]{1,0:T(8,128)(2,1)S(1)}, bf16[128,2048]{1,0:T(8,128)(2,1)S(1)}, u32[]{:S(2)}, u32[]{:S(2)}) collective-permute-start(bf16[128,2048]{1,0:T(8,128)(2,1)S(1)} %add_convert_fusion), channel_id=1, source_target_pairs={{0,2},{1,3},{2,6},{3,7},{6,4},{7,5},{4,0},{5,1},{8,10},{9,11},{10,... | collective-permute-start | bytes 1572872 | tf_op jit(solution)/shard_map/ppermute | solution.py:269
Sparse Core Ops, SparseCore 0:
  32.4 36.9 all-gather.2
where the time goes:
time: 209 us
  waiting for transfers between devices  93.1 us (45%)
  starting transfers between devices  50.7 us (24%)
  Pallas kernels  35.1 us (17%)
  between operations  14.5 us (7%)
  local copies, waits for them, and re-layouts  13.7 us (7%)
    ppermute x10, waiting for transfers between devices, to_next(): return lax.ppermute(value, 'cand', along)  65.6 us
    ppermute x10, starting transfers between devices, to_next(): return lax.ppermute(value, 'cand', along)  24.7 us
    ppermute x16, starting transfers between devices, flip(): return lax.ppermute(value, 'prod', [(q, q ^ r) for q in range(parts)])  23.5 us
    ppermute x16, waiting for transfers between devices, flip(): return lax.ppermute(value, 'prod', [(q, q ^ r) for q in range(parts)])  20.4 us
    pallas_call x4, Pallas kernels, query(): pl.pallas_call(functools.partial(query_kernel, len(weights), parts), out_...  10.6 us
    pallas_call x8, Pallas kernels, project(): pl.pallas_call(functools.partial(project_kernel, pieces), out_shape=[shap...  10.6 us
    unnamed x47, local copies, waits for them, and re-layouts  9.47 us
    pallas_call x4, Pallas kernels, attend(): pl.pallas_call(functools.partial(attend_kernel, order, step), out_shape=j...  9.01 us
  transfers between devices with their start and end apart: 39, of which 17 were waited for; matrix products, arithmetic and copies ran while one was open for 3% of the time, Pallas kernels for 16%

commit v1 on v0

--- a/solution.py
+++ b/solution.py
@@ -47,20 +47,20 @@
     )(ids, x)
 
 
-def key_value_kernel(parts, rows, tiles, tile_of, enc_ref, w_key, w_value, open_ref, *outs):
+def key_value_kernel(plan, parts, rows, tiles, enc_ref, w_key, w_value, open_ref, *outs):
     slots, height, block = enc_ref.shape
-    local = w_key.shape[1]
+    elen = slots * rows
     encoder = jnp.concatenate([enc_ref[slot, : parts * rows, :] for slot in range(slots)], axis=0)
-    for column, weight in ((0, w_key), (local, w_value)):
+    for which, weight in enumerate((w_key, w_value)):
         sums = jnp.dot(encoder, weight[...], preferred_element_type=jnp.float32)
-        for slot in range(slots):
-            for r in range(parts):
-                start = (slot * parts + r) * rows
-                outs[r][slot * rows : (slot + 1) * rows, column : column + local] = sums[
-                    start : start + rows
-                ].astype(outs[r].dtype)
-    elen = slots * rows
-    tile = lax.broadcasted_iota(jnp.int32, (1, elen), 1) // tile_of
+        for (kind, places, _), out in zip(plan, outs):
+            if kind != which:
+                continue
+            for index, r in enumerate(places):
+                for slot in range(slots):
+                    start, target = (slot * parts + r) * rows, index * elen + slot * rows
+                    out[target : target + rows, :] = sums[start : start + rows].astype(out.dtype)
+    tile = lax.broadcasted_iota(jnp.int32, (1, elen), 1) // TILE
     for slot in range(slots):
         seen = jnp.zeros((1, elen), jnp.float32)
         for t in range(tiles):
@@ -70,19 +70,16 @@
         open_ref[slot : slot + 1, :] = seen
 
 
-def key_value(gathered, w_key, w_value, parts, rows, tiles):
+def key_value(plan, gathered, w_key, w_value, parts, rows, tiles):
     slots, local = gathered.shape[0], w_key.shape[1]
     elen = slots * rows
     return pl.pallas_call(
-        functools.partial(key_value_kernel, parts, rows, tiles, TILE),
+        functools.partial(key_value_kernel, plan, parts, rows, tiles),
         out_shape=[jax.ShapeDtypeStruct((slots, elen), jnp.float32)]
-        + [
-            jax.ShapeDtypeStruct((elen, 2 * local), jnp.float32 if r == 0 else jnp.bfloat16)
-            for r in range(parts)
-        ],
+        + [jax.ShapeDtypeStruct((len(places) * elen, local), kept) for _, places, kept in plan],
         in_specs=[pl.BlockSpec(memory_space=pltpu.VMEM)] * 3,
-        out_specs=[pl.BlockSpec(memory_space=pltpu.VMEM)] * (parts + 1),
-        compiler_params=VMEM,
+        out_specs=[pl.BlockSpec(memory_space=pltpu.VMEM)] * (len(plan) + 1),
+        compiler_params=pltpu.CompilerParams(vmem_limit_bytes=58 * 1024 * 1024),
         cost_estimate=small(),
         name="key_value",
     )(gathered, w_key, w_value)
@@ -128,7 +125,7 @@
     )(ids, mine, sib, *weights)
 
 
-def attend_kernel(order, step, ids, query_ref, open_ref, kv_ref, out_ref):
+def attend_kernel(order, step, ids, query_ref, open_ref, key_ref, value_ref, out_ref):
     chips = len(order)
     chip, core = lax.div(ids[1], 2), lax.rem(ids[1], 2)
     source = chip
@@ -137,7 +134,7 @@
             source = jnp.where(chip == order[place], order[(place - step) % chips], source)
     who = (2 * source + core, 2 * source + 1 - core)
     clen = query_ref.shape[0] // 2
-    elen, local = kv_ref.shape[0], kv_ref.shape[1] // 2
+    elen, local = key_ref.shape
     is_open = (
         jnp.concatenate(
             [jnp.broadcast_to(open_ref[pl.ds(who[i], 1), :], (clen, elen)) for i in range(2)],
@@ -148,8 +145,7 @@
     lane = lax.broadcasted_iota(jnp.int32, (elen, LANES), 1) // HD
     for pair in range(local // LANES):
         columns = slice(pair * LANES, (pair + 1) * LANES)
-        keys = kv_ref[:, columns]
-        values = kv_ref[:, local + pair * LANES : local + (pair + 1) * LANES]
+        keys, values = key_ref[:, columns], value_ref[:, columns]
         context = None
         for half in range(LANES // HD):
             own = lane == half
@@ -175,17 +171,17 @@
         out_ref[:, columns] = context.astype(jnp.bfloat16)
 
 
-def attend(order, step, ids, queries, is_open, kv):
+def attend(order, step, ids, queries, is_open, keys, values):
     return pl.pallas_call(
         functools.partial(attend_kernel, order, step),
         out_shape=jax.ShapeDtypeStruct(queries.shape, jnp.bfloat16),
         in_specs=[pl.BlockSpec(memory_space=pltpu.SMEM)]
-        + [pl.BlockSpec(memory_space=pltpu.VMEM)] * 3,
+        + [pl.BlockSpec(memory_space=pltpu.VMEM)] * 4,
         out_specs=pl.BlockSpec(memory_space=pltpu.VMEM),
         compiler_params=VMEM,
         cost_estimate=small(),
         name="attend",
-    )(ids, queries, is_open, kv)
+    )(ids, queries, is_open, keys, values)
 
 
 def project_kernel(pieces, context_ref, *refs):
@@ -279,14 +275,13 @@
     clen, width = cand_states.shape[2:]
     states = cand_states.reshape(clen, width)
     pairs = [(states, to_sib(states))]
-    top = to_next(states[: clen // 2])
-
-    half = w_query.shape[0] // 2
-    if parts == 4:
-        upper, lower = w_query[:half], w_query[half:]
-        first = [flip(upper, 1), flip(lower, 2)]
-    else:
-        first = [flip(w_query, 1)]
+    states = to_next(states)
+
+    def corner(weight, first, second):
+        half = weight.shape[0] // 2
+        return [flip(first[:half], 2), flip(second[half:], 1)]
+
+    query_parts = [w_query] + [flip(w_query, r) for r in range(1, min(parts, 3))]
 
     rows = enc_rows.shape[1]
     block = width // parts
@@ -296,48 +291,71 @@
     flags = tile_mask.reshape(1, tiles, 1).astype(jnp.bfloat16)
     flags = jnp.broadcast_to(flags, (FLAG_ROWS, tiles, block // tiles)).reshape(FLAG_ROWS, block)
     piece = jnp.concatenate(columns + [flags], axis=0)
-    piece, top, first = lax.optimization_barrier((piece, top, first))
+    piece, states, query_parts = lax.optimization_barrier((piece, states, query_parts))
     gathered = lax.all_gather(piece, "cand", axis=0)
 
-    states = jnp.concatenate([top, to_next(states[clen // 2 :])], axis=0)
     pairs.append((states, to_sib(states)))
     for _ in range(2, chips):
         states = to_next(states)
         pairs.append((states, to_sib(states)))
     if parts == 4:
-        corner = [flip(first[0], 2), flip(first[1], 1)]
-        query_parts = [w_query, first[0], flip(lower, 1), flip(upper, 2), first[1]] + corner
+        query_parts += corner(*query_parts)
     else:
-        query_parts = [w_query, first[0]] + [flip(w_query, r) for r in range(2, parts)]
+        query_parts += [flip(w_query, r) for r in range(3, parts)]
 
     query_parts, w_out = lax.optimization_barrier((query_parts, w_out))
     out_parts = [w_out] + [flip(w_out, r) for r in range(1, parts if parts != 4 else 3)]
     if parts == 4:
-        half = w_out.shape[0] // 2
-        out_parts += [flip(out_parts[1][:half], 2), flip(out_parts[2][half:], 1)]
+        out_parts += corner(*out_parts)
     out_chunks = [out_parts[: parts // 2], out_parts[parts // 2 :]]
 
-    is_open, *sums = key_value(gathered, w_key, w_value, parts, rows, tiles)
-    kv = sums[0]
-    for r in range(1, parts):
-        kv = kv + flip(sums[r], r).astype(jnp.float32)
-    kv = kv.astype(jnp.bfloat16)
-
+    f32, bf16 = jnp.float32, jnp.bfloat16
+    elen = devices * rows
+    if parts == 4:
+        plan = [(0, (0,), f32), (0, (2,), f32), (0, (1, 3), bf16)]
+        plan += [(1, (0,), f32), (1, (1,), f32), (1, (2, 3), bf16)]
+    else:
+        plan = [(which, (r,), bf16 if r else f32) for which in range(2) for r in range(parts)]
+    is_open, *sums = key_value(plan, gathered, w_key, w_value, parts, rows, tiles)
+    if parts == 4:
+        (key, key_far, key_sent), (value, value_far, value_sent) = sums[:3], sums[3:]
+        came = lax.optimization_barrier((flip(key_sent, 1), flip(value_sent, 2)))
+        came = [rows_in.astype(f32) for rows_in in came]
+        far = [(key_far + came[0][elen:]).astype(bf16), (value_far + came[1][elen:]).astype(bf16)]
+        far = lax.optimization_barrier((flip(far[0], 2), flip(far[1], 1)))
+        projected = [
+            (own + near[:elen] + last.astype(f32)).astype(bf16)
+            for own, near, last in zip((key, value), came, far)
+        ]
+    else:
+        projected = []
+        for own, *others in (sums[:parts], sums[parts:]):
+            for r in range(1, parts):
+                own = own + flip(others[r - 1], r).astype(f32)
+            projected.append(own.astype(bf16))
+
+    steps = list(range(1, chips)) + [0]
     passed = [None] * len(out_chunks)
-    for step in list(range(1, chips)) + [0]:
-        queries = query(ids, *pairs[step], query_parts, parts)
-        context = attend(order, step, ids, queries, is_open, kv)
-        last = []
-        for chunk, weights in enumerate(out_chunks):
+    queries = query(ids, *pairs[steps[0]], query_parts, parts)
+    for index, step in enumerate(steps):
+        context = attend(order, step, ids, queries, is_open, *projected)
+        sums = []
+        for weights in out_chunks:
             mine, sib = project(context, weights)
-            other = to_sib(sib)
-            if step:
-                total = mine.astype(jnp.float32) + other.astype(jnp.float32)
-                if passed[chunk] is not None:
-                    total = total + passed[chunk].astype(jnp.float32)
-                passed[chunk] = to_next(total.astype(jnp.bfloat16))
-            else:
-                last += [mine, other, passed[chunk]]
+            sums.append((mine, to_sib(sib)))
+        if not step:
+            break
+        totals = []
+        for chunk, (mine, other) in enumerate(sums):
+            total = mine.astype(f32) + other.astype(f32)
+            if passed[chunk] is not None:
+                total = total + passed[chunk].astype(f32)
+            totals.append(total.astype(bf16))
+        queries = query(ids, *pairs[steps[index + 1]], query_parts, parts)
+        if not index:
+            totals, queries = lax.optimization_barrier((totals, queries))
+        passed = [to_next(total) for total in totals]
+    last = [part for (mine, other), came in zip(sums, passed) for part in (mine, other, came)]
     return finish(ids, counts, last, parts, width).reshape(cand_states.shape)
 
 

time: 209 us -> 230 us (1.10)
  waiting for transfers between devices: 93.1 us -> 144 us
  starting transfers between devices: 50.7 us -> 28.9 us
  local copies, waits for them, and re-layouts: 13.7 us -> 3.87 us
    ppermute x16 -> x15, waiting for transfers between devices: 20.4 us -> 51.5 us  [flip(): return lax.ppermute(value, 'prod', [(q, q ^ r) for q in range(parts)])]
    all_gather x1, waiting for transfers between devices: 7.05 us -> 28.3 us  [shards(): gathered = lax.all_gather(piece, 'cand', axis=0)]
    ppermute x10 -> x9, starting transfers between devices: 24.7 us -> 6.86 us  [to_next(): return lax.ppermute(value, 'cand', along)]
    unnamed x47 -> x28, local copies, waits for them, and re-layouts: 9.47 us -> 2.13 us
    pallas_call x8, Pallas kernels: 10.6 us -> 5.7 us  [project(): pl.pallas_call(functools.partial(project_kernel, pieces), out_shape=[shap...]
    ppermute x16 -> x15, starting transfers between devices: 23.5 us -> 19.4 us  [flip(): return lax.ppermute(value, 'prod', [(q, q ^ r) for q in range(parts)])]
    pallas_call x1, Pallas kernels: 2.32 us -> 5.82 us  [key_value(): pl.pallas_call(functools.partial(key_value_kernel, plan, parts, rows, til...]
    ppermute x10 -> x9, waiting for transfers between devices: 65.6 us -> 64 us  [to_next(): return lax.ppermute(value, 'cand', along)]
  transfers between devices with their start and end apart: 39 -> 37, of which waited for: 17 -> 17; matrix products, arithmetic and copies ran while one was open for 3% -> 2% of each run, Pallas kernels for 16% -> 14%
where the time goes in v1:
time: 230 us; the launch traced here: 229 us
  waiting for transfers between devices  144 us (63%)
  Pallas kernels  34.6 us (15%)
  starting transfers between devices  28.9 us (13%)
  between operations  14.5 us (6%)
  local copies, waits for them, and re-layouts  3.87 us (2%)
  other arithmetic  3.73 us (2%)
    ppermute x9, waiting for transfers between devices, to_next(): return lax.ppermute(value, 'cand', along)  64 us
    ppermute x15, waiting for transfers between devices, flip(): return lax.ppermute(value, 'prod', [(q, q ^ r) for q in range(parts)])  51.5 us
    all_gather x1, waiting for transfers between devices, shards(): gathered = lax.all_gather(piece, 'cand', axis=0)  28.3 us
    ppermute x15, starting transfers between devices, flip(): return lax.ppermute(value, 'prod', [(q, q ^ r) for q in range(parts)])  19.4 us
    pallas_call x4, Pallas kernels, query(): pl.pallas_call(functools.partial(query_kernel, len(weights), parts), out_...  11.6 us
    pallas_call x4, Pallas kernels, attend(): pl.pallas_call(functools.partial(attend_kernel, order, step), out_shape=j...  9 us
    ppermute x9, starting transfers between devices, to_next(): return lax.ppermute(value, 'cand', along)  6.86 us
    pallas_call x1, Pallas kernels, key_value(): pl.pallas_call(functools.partial(key_value_kernel, plan, parts, rows, til...  5.82 us
  transfers between devices with their start and end apart: 37, of which 17 were waited for; matrix products, arithmetic and copies ran while one was open for 2% of the time, Pallas kernels for 14%

profile of v1, /device:TPU:0, one launch (start us, length us, event | category | flops | bytes accessed | tf_op | source)
XLA Modules:
  0.0 229.5 jit_solution(14272106119786538990)
XLA Ops:
  6.5 2.9 %collective-permute-start.5 = (bf16[1024,512]{1,0:T(8,128)(2,1)}, bf16[1024,512]{1,0:T(8,128)(2,1)S(1)}, u32[]{:S(2)}, u32[]{:S(2)}) collective-permute-start(bf16[1024,512]{1,0:T(8,128)(2,1)} %refs_0_.6), channel_id=1, source_target_pairs={{0,8},{8,0},{16,24},{24,16},{1,9},{9,1},{17,25},{25,17},{2,10},{10... | collective-permute-start | bytes 3145736 | tf_op jit(solution)/shard_map/ppermute | solution.py:271
  9.5 1.5 collective-permute-start.6
  11.1 0.9 copy-done.5
  12.0 0.6 columns.1
  12.6 0.6 collective-permute-start.1
  13.2 2.0 collective-permute-start.4
  15.3 0.7 convert_bitcast_fusion
  16.0 18.2 %collective-permute-done.1 = bf16[32,1024]{1,0:T(8,128)(2,1)S(1)} collective-permute-done((bf16[32,1024]{1,0:T(8,128)(2,1)S(1)}, bf16[32,1024]{1,0:T(8,128)(2,1)S(1)}, u32[]{:S(2)}, u32[]{:S(2)}) %collective-permute-start.1) | collective-permute-done | bytes 65568 | tf_op jit(solution)/shard_map/ppermute | solution.py:271
  34.2 2.7 %collective-permute-start.3 = (bf16[32,1024]{1,0:T(8,128)(2,1)S(1)}, bf16[32,1024]{1,0:T(8,128)(2,1)S(1)}, u32[]{:S(2)}, u32[]{:S(2)}) collective-permute-start(bf16[32,1024]{1,0:T(8,128)(2,1)S(1)} %get-tuple-element.53), channel_id=1, source_target_pairs={{0,24},{8,16},{16,8},{24,0},{1,25},{9,17},{17,9},{25,1},{2,26},{10... | collective-permute-start | bytes 196616 | tf_op jit(solution)/shard_map/ppermute | solution.py:271
  37.0 2.4 %collective-permute-done.3 = bf16[32,1024]{1,0:T(8,128)(2,1)S(1)} collective-permute-done((bf16[32,1024]{1,0:T(8,128)(2,1)S(1)}, bf16[32,1024]{1,0:T(8,128)(2,1)S(1)}, u32[]{:S(2)}, u32[]{:S(2)}) %collective-permute-start.3) | collective-permute-done | bytes 65568 | tf_op jit(solution)/shard_map/ppermute | solution.py:271
  39.5 0.7 copy-done.10
  40.2 0.8 slice.24
  41.0 1.8 collective-permute-start.7
  42.8 0.8 slice.25
  43.6 1.5 collective-permute-start.8
  45.1 28.3 %all-gather.3.cloned.1.call-done = bf16[1152,1024]{1,0:T(8,128)(2,1)} async-done(((bf16[144,1024]{1,0:T(8,128)(2,1)}), bf16[1152,1024]{1,0:T(8,128)(2,1)}) %all-gather.3.cloned.1.call-update) | async-done | bytes 2359312 | tf_op jit(solution)/shard_map/all_gather | solution.py:295
  73.5 5.8 %key_value.1 = (f32[8,256]{1,0:T(8,128)}, f32[256,512]{1,0:T(8,128)}, f32[256,512]{1,0:T(8,128)}, bf16[512,512]{1,0:T(8,128)(2,1)}, f32[256,512]{1,0:T(8,128)}, ...) custom-call(bf16[8,144,1024]{2,1,0:T(8,128)(2,1)} %bitcast.15, bf16[1024,512]{1,0:T(8,128)(2,1)} %w_key.1, ...), custom_call_target="tpu_custom_call" | custom-call | flops 1 | bytes 1 | tf_op jit(solution)/shard_map/key_value/pallas_call | solution.py:76
  79.3 1.5 collective-permute-start.10
  80.8 1.0 collective-permute-start.15
  81.8 1.5 collective-permute-start.9
  83.3 0.6 collective-permute-start.13
  83.9 0.6 collective-permute-start.21
  84.4 9.8 %collective-permute-done.10 = bf16[512,512]{1,0:T(8,128)(2,1)S(1)} collective-permute-done((bf16[512,512]{1,0:T(8,128)(2,1)}, bf16[512,512]{1,0:T(8,128)(2,1)S(1)}, u32[]{:S(2)}, u32[]{:S(2)}) %collective-permute-start.10) | collective-permute-done | bytes 524320 | tf_op jit(solution)/shard_map/ppermute | solution.py:271
  94.3 2.6 %collective-permute-done.9 = bf16[512,512]{1,0:T(8,128)(2,1)S(1)} collective-permute-done((bf16[512,512]{1,0:T(8,128)(2,1)}, bf16[512,512]{1,0:T(8,128)(2,1)S(1)}, u32[]{:S(2)}, u32[]{:S(2)}) %collective-permute-start.9) | collective-permute-done | bytes 524320 | tf_op jit(solution)/shard_map/ppermute | solution.py:271
  97.0 1.1 fusion.2
  98.1 1.5 collective-permute-start.12
  99.9 6.8 %collective-permute-done.15.mine = bf16[128,4096]{1,0:T(8,128)(2,1)S(1)} collective-permute-done((bf16[128,4096]{1,0:T(8,128)(2,1)S(1)}, bf16[128,4096]{1,0:T(8,128)(2,1)S(1)}, u32[]{:S(2)}, u32[]{:S(2)}) %collective-permute-start.15) | collective-permute-done | bytes 1048608 | tf_op jit(solution)/shard_map/ppermute | solution.py:265
  106.7 0.6 collective-permute-start.11
  107.2 12.1 %collective-permute-done.13.refs_1_ = bf16[512,1024]{1,0:T(8,128)(2,1)S(1)} collective-permute-done((bf16[512,1024]{1,0:T(8,128)(2,1)S(1)}, bf16[512,1024]{1,0:T(8,128)(2,1)S(1)}, u32[]{:S(2)}, u32[]{:S(2)}) %collective-permute-start.13) | collective-permute-done | bytes 1048608 | tf_op jit(solution)/shard_map/ppermute | solution.py:271
  119.3 1.1 collective-permute-start.16
  120.4 0.7 collective-permute-start.22
  121.1 1.5 collective-permute-start.23
  122.6 2.3 collective-permute-done.12
  124.9 2.9 %query.6.query_ref = bf16[256,512]{1,0:T(8,128)(2,1)S(1)} custom-call(s32[2]{0:T(128)S(1)} %pad_add_fusion.ids, bf16[128,4096]{1,0:T(8,128)(2,1)S(1)} %copy-done.4, bf16[128,4096]{1,0:T(8,128)(2,1)S(1)} %collective-permute-done.19.sib, bf16[1024,512]{1,0:T(8,128)(2,1)S(1)} %copy-done.1, bf16[1024,512]{1,0:T(8,128)(2,1)S(1)} %collective-permute-done.5.refs_1_, ...), custom_call_target="tpu_custom_call" | custom-call | flops 1 | bytes 1 | tf_op jit(solution)/shard_map/query/pallas_call | solution.py:116
  128.5 2.3 attend.6.context_ref
  130.8 2.1 collective-permute-done.22.refs_1_
  132.9 1.9 collective-permute-done.23.refs_2_
  134.8 0.7 project.11
  135.6 0.7 project.10
  136.3 0.6 collective-permute-start.20
  136.9 5.8 %collective-permute-done.16.mine = bf16[128,4096]{1,0:T(8,128)(2,1)S(1)} collective-permute-done((bf16[128,4096]{1,0:T(8,128)(2,1)S(1)}, bf16[128,4096]{1,0:T(8,128)(2,1)S(1)}, u32[]{:S(2)}, u32[]{:S(2)}) %collective-permute-start.16) | collective-permute-done | bytes 1048608 | tf_op jit(solution)/shard_map/ppermute | solution.py:265
  142.8 2.9 %query.7.query_ref = bf16[256,512]{1,0:T(8,128)(2,1)S(1)} custom-call(s32[2]{0:T(128)S(1)} %pad_add_fusion.ids, bf16[128,4096]{1,0:T(8,128)(2,1)S(1)} %collective-permute-done.15.mine, bf16[128,4096]{1,0:T(8,128)(2,1)S(1)} %collective-permute-done.25.sib, bf16[1024,512]{1,0:T(8,128)(2,1)S(1)} %copy-done.1, ...), custom_call_target="tpu_custom_call" | custom-call | flops 1 | bytes 1 | tf_op jit(solution)/shard_map/query/pallas_call | solution.py:116
  146.0 2.2 attend.7.context_ref
  148.2 0.7 project.15
  148.9 0.6 collective-permute-start.32
  149.9 0.7 project.12
  150.6 0.4 collective-permute-start.26
  151.0 2.4 %collective-permute-start.27 = (bf16[128,2048]{1,0:T(8,128)(2,1)S(1)}, bf16[128,2048]{1,0:T(8,128)(2,1)S(1)}, u32[]{:S(2)}, u32[]{:S(2)}) collective-permute-start(bf16[128,2048]{1,0:T(8,128)(2,1)S(1)} %add_convert_fusion.5), channel_id=1, source_target_pairs={{0,2},{1,3},{2,6},{3,7},{6,4},{7,5},{4,0},{5,1},{8,10},{9,11},{10,... | collective-permute-start | bytes 1572872 | tf_op jit(solution)/shard_map/ppermute | solution.py:265
  153.3 2.9 %query.5.query_ref = bf16[256,512]{1,0:T(8,128)(2,1)S(1)} custom-call(s32[2]{0:T(128)S(1)} %pad_add_fusion.ids, bf16[128,4096]{1,0:T(8,128)(2,1)S(1)} %collective-permute-done.16.mine, bf16[128,4096]{1,0:T(8,128)(2,1)S(1)} %collective-permute-done.17.sib, bf16[1024,512]{1,0:T(8,128)(2,1)S(1)} %copy-done.1, ...), custom_call_target="tpu_custom_call" | custom-call | flops 1 | bytes 1 | tf_op jit(solution)/shard_map/query/pallas_call | solution.py:116
  156.2 2.2 attend.5.context_ref
  158.5 0.7 project.14
  159.2 0.7 project.9
  160.0 5.2 %collective-permute-done.33 = bf16[128,2048]{1,0:T(8,128)(2,1)S(1)} collective-permute-done((bf16[128,2048]{1,0:T(8,128)(2,1)S(1)}, bf16[128,2048]{1,0:T(8,128)(2,1)S(1)}, u32[]{:S(2)}, u32[]{:S(2)}) %collective-permute-start.33) | collective-permute-done | bytes 524320 | tf_op jit(solution)/shard_map/ppermute | solution.py:265
  165.6 10.8 %collective-permute-done.27 = bf16[128,2048]{1,0:T(8,128)(2,1)S(1)} collective-permute-done((bf16[128,2048]{1,0:T(8,128)(2,1)S(1)}, bf16[128,2048]{1,0:T(8,128)(2,1)S(1)}, u32[]{:S(2)}, u32[]{:S(2)}) %collective-permute-start.27) | collective-permute-done | bytes 524320 | tf_op jit(solution)/shard_map/ppermute | solution.py:265
  176.7 2.9 %query.4.query_ref = bf16[256,512]{1,0:T(8,128)(2,1)S(1)} custom-call(s32[2]{0:T(128)S(1)} %pad_add_fusion.ids, bf16[128,4096]{1,0:T(8,128)(2,1)S(1)} %bitcast.13, bf16[128,4096]{1,0:T(8,128)(2,1)S(1)} %collective-permute-done.sib, bf16[1024,512]{1,0:T(8,128)(2,1)S(1)} %copy-done.1, bf16[1024,512]{1,0:T(8,128)(2,1)S(1)} %collective-permute-done.5.refs_1_, ...), custom_call_target="tpu_custom_call" | custom-call | flops 1 | bytes 1 | tf_op jit(solution)/shard_map/query/pallas_call | solution.py:116
  179.7 2.3 attend.4.context_ref
  181.9 0.7 project.13
  182.7 0.7 project.8
  183.5 0.6 collective-permute-start.14
  184.0 3.6 %collective-permute-done.34 = bf16[128,2048]{1,0:T(8,128)(2,1)S(1)} collective-permute-done((bf16[128,2048]{1,0:T(8,128)(2,1)S(1)}, bf16[128,2048]{1,0:T(8,128)(2,1)S(1)}, u32[]{:S(2)}, u32[]{:S(2)}) %collective-permute-start.34) | collective-permute-done | bytes 524320 | tf_op jit(solution)/shard_map/ppermute | solution.py:265
  188.0 10.9 %collective-permute-done.28 = bf16[128,2048]{1,0:T(8,128)(2,1)S(1)} collective-permute-done((bf16[128,2048]{1,0:T(8,128)(2,1)S(1)}, bf16[128,2048]{1,0:T(8,128)(2,1)S(1)}, u32[]{:S(2)}, u32[]{:S(2)}) %collective-permute-start.28) | collective-permute-done | bytes 524320 | tf_op jit(solution)/shard_map/ppermute | solution.py:265
  199.9 10.3 %collective-permute-done.35.refs_5_ = bf16[128,2048]{1,0:T(8,128)(2,1)S(1)} collective-permute-done((bf16[128,2048]{1,0:T(8,128)(2,1)S(1)}, bf16[128,2048]{1,0:T(8,128)(2,1)S(1)}, u32[]{:S(2)}, u32[]{:S(2)}) %collective-permute-start.35) | collective-permute-done | bytes 524320 | tf_op jit(solution)/shard_map/ppermute | solution.py:265
  210.1 10.5 %collective-permute-done.29.refs_2_ = bf16[128,2048]{1,0:T(8,128)(2,1)S(1)} collective-permute-done((bf16[128,2048]{1,0:T(8,128)(2,1)S(1)}, bf16[128,2048]{1,0:T(8,128)(2,1)S(1)}, u32[]{:S(2)}, u32[]{:S(2)}) %collective-permute-start.29) | collective-permute-done | bytes 524320 | tf_op jit(solution)/shard_map/ppermute | solution.py:265
  220.7 2.0 finish.1
  (76 shorter events, 3.5 us)
Async XLA Ops:
  6.5 66.9 %all-gather.3.cloned.1.call-start = ((), (), s32[]{:S(2)}) async-start(), calls=%async_computation | async-start | bytes 2654208 | tf_op jit(solution)/shard_map/all_gather | solution.py:295
  6.5 32.9 %collective-permute-start.5 = (bf16[1024,512]{1,0:T(8,128)(2,1)}, bf16[1024,512]{1,0:T(8,128)(2,1)S(1)}, u32[]{:S(2)}, u32[]{:S(2)}) collective-permute-start(bf16[1024,512]{1,0:T(8,128)(2,1)} %refs_0_.6), channel_id=1, source_target_pairs={{0,8},{8,0},{16,24},{24,16},{1,9},{9,1},{17,25},{25,17},{2,10},{10... | collective-permute-start | bytes 3145736 | tf_op jit(solution)/shard_map/ppermute | solution.py:271
  9.5 30.0 %collective-permute-start.6 = (bf16[1024,512]{1,0:T(8,128)(2,1)}, bf16[1024,512]{1,0:T(8,128)(2,1)S(1)}, u32[]{:S(2)}, u32[]{:S(2)}) collective-permute-start(bf16[1024,512]{1,0:T(8,128)(2,1)} %refs_0_.6), channel_id=1, source_target_pairs={{0,16},{8,24},{16,0},{24,8},{1,17},{9,25},{17,1},{25,9},{2,18},{10... | collective-permute-start | bytes 3145736 | tf_op jit(solution)/shard_map/ppermute | solution.py:271
  11.1 0.9 copy-start.5
  12.6 21.7 %collective-permute-start.1 = (bf16[32,1024]{1,0:T(8,128)(2,1)S(1)}, bf16[32,1024]{1,0:T(8,128)(2,1)S(1)}, u32[]{:S(2)}, u32[]{:S(2)}) collective-permute-start(bf16[32,1024]{1,0:T(8,128)(2,1)S(1)} %get-tuple-element.51), channel_id=1, source_target_pairs={{0,8},{8,0},{16,24},{24,16},{1,9},{9,1},{17,25},{25,17},{2,10},{10... | collective-permute-start | bytes 196616 | tf_op jit(solution)/shard_map/ppermute | solution.py:271
  13.2 23.8 %collective-permute-start.2 = (bf16[32,1024]{1,0:T(8,128)(2,1)S(1)}, bf16[32,1024]{1,0:T(8,128)(2,1)S(1)}, u32[]{:S(2)}, u32[]{:S(2)}) collective-permute-start(bf16[32,1024]{1,0:T(8,128)(2,1)S(1)} %get-tuple-element.52), channel_id=1, source_target_pairs={{0,16},{8,24},{16,0},{24,8},{1,17},{9,25},{17,1},{25,9},{2,18},{10... | collective-permute-start | bytes 196616 | tf_op jit(solution)/shard_map/ppermute | solution.py:271
  13.2 26.2 %collective-permute-start.4 = (bf16[128,4096]{1,0:T(8,128)(2,1)}, bf16[128,4096]{1,0:T(8,128)(2,1)S(1)}, u32[]{:S(2)}, u32[]{:S(2)}) collective-permute-start(bf16[128,4096]{1,0:T(8,128)(2,1)} %bitcast.11), channel_id=1, source_target_pairs={{0,2},{1,3},{2,6},{3,7},{6,4},{7,5},{4,0},{5,1},{8,10},{9,11},{10,... | collective-permute-start | bytes 3145736 | tf_op jit(solution)/shard_map/ppermute | solution.py:265
  34.2 5.2 %collective-permute-start.3 = (bf16[32,1024]{1,0:T(8,128)(2,1)S(1)}, bf16[32,1024]{1,0:T(8,128)(2,1)S(1)}, u32[]{:S(2)}, u32[]{:S(2)}) collective-permute-start(bf16[32,1024]{1,0:T(8,128)(2,1)S(1)} %get-tuple-element.53), channel_id=1, source_target_pairs={{0,24},{8,16},{16,8},{24,0},{1,25},{9,17},{17,9},{25,1},{2,26},{10... | collective-permute-start | bytes 196616 | tf_op jit(solution)/shard_map/ppermute | solution.py:271
  39.4 0.7 copy-start.10
  39.4 3.3 %copy-start.3 = (bf16[128,4096]{1,0:T(8,128)(2,1)}, bf16[128,4096]{1,0:T(8,128)(2,1)S(1)}, u32[]{:S(2)}) copy-start(bf16[128,4096]{1,0:T(8,128)(2,1)S(1)} %collective-permute-done.4.mine) | copy-start | bytes 3145732
  41.0 42.2 %collective-permute-start.7 = (bf16[512,512]{1,0:T(8,128)(2,1)}, bf16[512,512]{1,0:T(8,128)(2,1)}, u32[]{:S(2)}, u32[]{:S(2)}) collective-permute-start(bf16[512,512]{1,0:T(8,128)(2,1)} %slice.24), channel_id=1, source_target_pairs={{0,16},{8,24},{16,0},{24,8},{1,17},{9,25},{17,1},{25,9},{2,18},{10... | collective-permute-start | bytes 1572872 | tf_op jit(solution)/shard_map/ppermute | solution.py:271
  43.6 39.6 %copy-start = (bf16[512,1024]{1,0:T(8,128)(2,1)S(1)}, bf16[512,1024]{1,0:T(8,128)(2,1)}, u32[]{:S(2)}) copy-start(bf16[512,1024]{1,0:T(8,128)(2,1)} %refs_0_.7) | copy-start | bytes 3145732
  43.6 39.6 %collective-permute-start.8 = (bf16[512,512]{1,0:T(8,128)(2,1)}, bf16[512,512]{1,0:T(8,128)(2,1)}, u32[]{:S(2)}, u32[]{:S(2)}) collective-permute-start(bf16[512,512]{1,0:T(8,128)(2,1)} %slice.25), channel_id=1, source_target_pairs={{0,8},{8,0},{16,24},{24,16},{1,9},{9,1},{17,25},{25,17},{2,10},{10... | collective-permute-start | bytes 1572872 | tf_op jit(solution)/shard_map/ppermute | solution.py:271
  73.5 7.3 %copy-start.4 = (bf16[128,4096]{1,0:T(8,128)(2,1)S(1)}, bf16[128,4096]{1,0:T(8,128)(2,1)}, u32[]{:S(2)}) copy-start(bf16[128,4096]{1,0:T(8,128)(2,1)} %copy-done.3) | copy-start | bytes 3145732
  79.3 20.5 %copy-start.7 = (f32[256,512]{1,0:T(8,128)S(1)}, f32[256,512]{1,0:T(8,128)}, u32[]{:S(2)}) copy-start(f32[256,512]{1,0:T(8,128)} %get-tuple-element.68) | copy-start | bytes 1572868
  79.3 15.0 %collective-permute-start.10 = (bf16[512,512]{1,0:T(8,128)(2,1)}, bf16[512,512]{1,0:T(8,128)(2,1)S(1)}, u32[]{:S(2)}, u32[]{:S(2)}) collective-permute-start(bf16[512,512]{1,0:T(8,128)(2,1)} %get-tuple-element.66), channel_id=1, source_target_pairs={{0,16},{8,24},{16,0},{24,8},{1,17},{9,25},{17,1},{25,9},{2,18},{10... | collective-permute-start | bytes 1572872 | tf_op jit(solution)/shard_map/ppermute | solution.py:271
  80.8 25.9 %collective-permute-start.15 = (bf16[128,4096]{1,0:T(8,128)(2,1)S(1)}, bf16[128,4096]{1,0:T(8,128)(2,1)S(1)}, u32[]{:S(2)}, u32[]{:S(2)}) collective-permute-start(bf16[128,4096]{1,0:T(8,128)(2,1)S(1)} %copy-done.4), channel_id=1, source_target_pairs={{0,2},{1,3},{2,6},{3,7},{6,4},{7,5},{4,0},{5,1},{8,10},{9,11},{10,... | collective-permute-start | bytes 3145736 | tf_op jit(solution)/shard_map/ppermute | solution.py:265
  81.8 15.0 %collective-permute-start.9 = (bf16[512,512]{1,0:T(8,128)(2,1)}, bf16[512,512]{1,0:T(8,128)(2,1)S(1)}, u32[]{:S(2)}, u32[]{:S(2)}) collective-permute-start(bf16[512,512]{1,0:T(8,128)(2,1)} %get-tuple-element.65), channel_id=1, source_target_pairs={{0,8},{8,0},{16,24},{24,16},{1,9},{9,1},{17,25},{25,17},{2,10},{10... | collective-permute-start | bytes 1572872 | tf_op jit(solution)/shard_map/ppermute | solution.py:271
  83.3 36.0 %collective-permute-start.13 = (bf16[512,1024]{1,0:T(8,128)(2,1)S(1)}, bf16[512,1024]{1,0:T(8,128)(2,1)S(1)}, u32[]{:S(2)}, u32[]{:S(2)}) collective-permute-start(bf16[512,1024]{1,0:T(8,128)(2,1)S(1)} %copy-done), channel_id=1, source_target_pairs={{0,8},{8,0},{16,24},{24,16},{1,9},{9,1},{17,25},{25,17},{2,10},{10... | collective-permute-start | bytes 3145736 | tf_op jit(solution)/shard_map/ppermute | solution.py:271
  83.9 36.5 %collective-permute-start.21 = (bf16[512,1024]{1,0:T(8,128)(2,1)S(1)}, bf16[512,1024]{1,0:T(8,128)(2,1)S(1)}, u32[]{:S(2)}, u32[]{:S(2)}) collective-permute-start(bf16[512,1024]{1,0:T(8,128)(2,1)S(1)} %copy-done), channel_id=1, source_target_pairs={{0,16},{8,24},{16,0},{24,8},{1,17},{9,25},{17,1},{25,9},{2,18},{10... | collective-permute-start | bytes 3145736 | tf_op jit(solution)/shard_map/ppermute | solution.py:271
  94.3 26.9 %collective-permute-start.19 = (bf16[128,4096]{1,0:T(8,128)(2,1)S(1)}, bf16[128,4096]{1,0:T(8,128)(2,1)S(1)}, u32[]{:S(2)}, u32[]{:S(2)}) collective-permute-start(bf16[128,4096]{1,0:T(8,128)(2,1)S(1)} %copy-done.4), channel_id=1, source_target_pairs={{0,1},{1,0},{2,3},{3,2},{4,5},{5,4},{6,7},{7,6},{8,9},{9,8},{10,11... | collective-permute-start | bytes 3145736 | tf_op jit(solution)/shard_map/ppermute | solution.py:268
  98.1 26.8 %copy-start.1 = (bf16[1024,512]{1,0:T(8,128)(2,1)S(1)}, bf16[1024,512]{1,0:T(8,128)(2,1)}, u32[]{:S(2)}) copy-start(bf16[1024,512]{1,0:T(8,128)(2,1)} %refs_0_.6) | copy-start | bytes 3145732
  98.1 26.8 %collective-permute-start.12 = (bf16[256,512]{1,0:T(8,128)(2,1)S(1)}, bf16[256,512]{1,0:T(8,128)(2,1)S(1)}, u32[]{:S(2)}, u32[]{:S(2)}) collective-permute-start(bf16[256,512]{1,0:T(8,128)(2,1)S(1)} %fusion.2), channel_id=1, source_target_pairs={{0,8},{8,0},{16,24},{24,16},{1,9},{9,1},{17,25},{25,17},{2,10},{10... | collective-permute-start | bytes 786440 | tf_op jit(solution)/shard_map/ppermute | solution.py:271
  106.7 21.1 %collective-permute-start.11 = (bf16[256,512]{1,0:T(8,128)(2,1)S(1)}, bf16[256,512]{1,0:T(8,128)(2,1)S(1)}, u32[]{:S(2)}, u32[]{:S(2)}) collective-permute-start(bf16[256,512]{1,0:T(8,128)(2,1)S(1)} %fusion.3), channel_id=1, source_target_pairs={{0,16},{8,24},{16,0},{24,8},{1,17},{9,25},{17,1},{25,9},{2,18},{10... | collective-permute-start | bytes 786440 | tf_op jit(solution)/shard_map/ppermute | solution.py:271
  119.3 23.5 %collective-permute-start.16 = (bf16[128,4096]{1,0:T(8,128)(2,1)S(1)}, bf16[128,4096]{1,0:T(8,128)(2,1)S(1)}, u32[]{:S(2)}, u32[]{:S(2)}) collective-permute-start(bf16[128,4096]{1,0:T(8,128)(2,1)S(1)} %collective-permute-done.15.mine), channel_id=1, source_target_pairs={{0,2},{1,3},{2,6},{3,7},{6,4},{7,5},{4,0},{5,1},{8,10},{9,11},{10,... | collective-permute-start | bytes 3145736 | tf_op jit(solution)/shard_map/ppermute | solution.py:265
  120.4 12.5 %collective-permute-start.22 = (bf16[256,1024]{1,0:T(8,128)(2,1)S(1)}, bf16[256,1024]{1,0:T(8,128)(2,1)S(1)}, u32[]{:S(2)}, u32[]{:S(2)}) collective-permute-start(bf16[256,1024]{1,0:T(8,128)(2,1)S(1)} %slice.36), channel_id=1, source_target_pairs={{0,16},{8,24},{16,0},{24,8},{1,17},{9,25},{17,1},{25,9},{2,18},{10... | collective-permute-start | bytes 1572872 | tf_op jit(solution)/shard_map/ppermute | solution.py:271
  121.1 6.7 %copy-start.8 = (f32[256,512]{1,0:T(8,128)S(1)}, f32[256,512]{1,0:T(8,128)}, u32[]{:S(2)}) copy-start(f32[256,512]{1,0:T(8,128)} %get-tuple-element.64) | copy-start | bytes 1572868
  121.1 6.7 %copy-start.9 = (f32[256,512]{1,0:T(8,128)S(1)}, f32[256,512]{1,0:T(8,128)}, u32[]{:S(2)}) copy-start(f32[256,512]{1,0:T(8,128)} %get-tuple-element.72) | copy-start | bytes 1572868
  121.1 13.7 %collective-permute-start.23 = (bf16[256,1024]{1,0:T(8,128)(2,1)S(1)}, bf16[256,1024]{1,0:T(8,128)(2,1)S(1)}, u32[]{:S(2)}, u32[]{:S(2)}) collective-permute-start(bf16[256,1024]{1,0:T(8,128)(2,1)S(1)} %slice.37), channel_id=1, source_target_pairs={{0,8},{8,0},{16,24},{24,16},{1,9},{9,1},{17,25},{25,17},{2,10},{10... | collective-permute-start | bytes 1572872 | tf_op jit(solution)/shard_map/ppermute | solution.py:271
  124.9 17.8 %collective-permute-start.25 = (bf16[128,4096]{1,0:T(8,128)(2,1)S(1)}, bf16[128,4096]{1,0:T(8,128)(2,1)S(1)}, u32[]{:S(2)}, u32[]{:S(2)}) collective-permute-start(bf16[128,4096]{1,0:T(8,128)(2,1)S(1)} %collective-permute-done.15.mine), channel_id=1, source_target_pairs={{0,1},{1,0},{2,3},{3,2},{4,5},{5,4},{6,7},{7,6},{8,9},{9,8},{10,11... | collective-permute-start | bytes 3145736 | tf_op jit(solution)/shard_map/ppermute | solution.py:268
  127.8 0.7 copy-start.6
  135.5 10.1 %collective-permute-start.24 = (bf16[128,2048]{1,0:T(8,128)(2,1)S(1)}, bf16[128,2048]{1,0:T(8,128)(2,1)S(1)}, u32[]{:S(2)}, u32[]{:S(2)}) collective-permute-start(bf16[128,2048]{1,0:T(8,128)(2,1)S(1)} %get-tuple-element.83), channel_id=1, source_target_pairs={{0,1},{1,0},{2,3},{3,2},{4,5},{5,4},{6,7},{7,6},{8,9},{9,8},{10,11... | collective-permute-start | bytes 1572872 | tf_op jit(solution)/shard_map/ppermute | solution.py:268
  136.3 9.5 %collective-permute-start.20 = (bf16[128,2048]{1,0:T(8,128)(2,1)S(1)}, bf16[128,2048]{1,0:T(8,128)(2,1)S(1)}, u32[]{:S(2)}, u32[]{:S(2)}) collective-permute-start(bf16[128,2048]{1,0:T(8,128)(2,1)S(1)} %get-tuple-element.81), channel_id=1, source_target_pairs={{0,1},{1,0},{2,3},{3,2},{4,5},{5,4},{6,7},{7,6},{8,9},{9,8},{10,11... | collective-permute-start | bytes 1572872 | tf_op jit(solution)/shard_map/ppermute | solution.py:268
  142.7 8.2 %collective-permute-start.17 = (bf16[128,4096]{1,0:T(8,128)(2,1)S(1)}, bf16[128,4096]{1,0:T(8,128)(2,1)S(1)}, u32[]{:S(2)}, u32[]{:S(2)}) collective-permute-start(bf16[128,4096]{1,0:T(8,128)(2,1)S(1)} %collective-permute-done.16.mine), channel_id=1, source_target_pairs={{0,1},{1,0},{2,3},{3,2},{4,5},{5,4},{6,7},{7,6},{8,9},{9,8},{10,11... | collective-permute-start | bytes 3145736 | tf_op jit(solution)/shard_map/ppermute | solution.py:268
  145.8 3.8 %copy-start.2 = (bf16[1,1,128,4096]{3,2,1,0:T(8,128)(2,1)S(1)}, bf16[1,1,128,4096]{3,2,1,0:T(8,128)(2,1)}, u32[]{:S(2)}) copy-start(bf16[1,1,128,4096]{3,2,1,0:T(8,128)(2,1)} %param.8) | copy-start | bytes 3145732
  148.9 11.0 %collective-permute-start.32 = (bf16[128,2048]{1,0:T(8,128)(2,1)S(1)}, bf16[128,2048]{1,0:T(8,128)(2,1)S(1)}, u32[]{:S(2)}, u32[]{:S(2)}) collective-permute-start(bf16[128,2048]{1,0:T(8,128)(2,1)S(1)} %get-tuple-element.93), channel_id=1, source_target_pairs={{0,1},{1,0},{2,3},{3,2},{4,5},{5,4},{6,7},{7,6},{8,9},{9,8},{10,11... | collective-permute-start | bytes 1572872 | tf_op jit(solution)/shard_map/ppermute | solution.py:268
  149.5 15.7 %collective-permute-start.33 = (bf16[128,2048]{1,0:T(8,128)(2,1)S(1)}, bf16[128,2048]{1,0:T(8,128)(2,1)S(1)}, u32[]{:S(2)}, u32[]{:S(2)}) collective-permute-start(bf16[128,2048]{1,0:T(8,128)(2,1)S(1)} %add_convert_fusion.4), channel_id=1, source_target_pairs={{0,2},{1,3},{2,6},{3,7},{6,4},{7,5},{4,0},{5,1},{8,10},{9,11},{10,... | collective-permute-start | bytes 1572872 | tf_op jit(solution)/shard_map/ppermute | solution.py:265
  149.7 27.1 %collective-permute-start = (bf16[128,4096]{1,0:T(8,128)(2,1)S(1)}, bf16[128,4096]{1,0:T(8,128)(2,1)S(1)}, u32[]{:S(2)}, u32[]{:S(2)}) collective-permute-start(bf16[128,4096]{1,0:T(8,128)(2,1)S(1)} %bitcast.12), channel_id=1, source_target_pairs={{0,1},{1,0},{2,3},{3,2},{4,5},{5,4},{6,7},{7,6},{8,9},{9,8},{10,11... | collective-permute-start | bytes 3145736 | tf_op jit(solution)/shard_map/ppermute | solution.py:268
  150.6 14.9 %collective-permute-start.26 = (bf16[128,2048]{1,0:T(8,128)(2,1)S(1)}, bf16[128,2048]{1,0:T(8,128)(2,1)S(1)}, u32[]{:S(2)}, u32[]{:S(2)}) collective-permute-start(bf16[128,2048]{1,0:T(8,128)(2,1)S(1)} %get-tuple-element.86), channel_id=1, source_target_pairs={{0,1},{1,0},{2,3},{3,2},{4,5},{5,4},{6,7},{7,6},{8,9},{9,8},{10,11... | collective-permute-start | bytes 1572872 | tf_op jit(solution)/shard_map/ppermute | solution.py:268
  151.0 25.5 %collective-permute-start.27 = (bf16[128,2048]{1,0:T(8,128)(2,1)S(1)}, bf16[128,2048]{1,0:T(8,128)(2,1)S(1)}, u32[]{:S(2)}, u32[]{:S(2)}) collective-permute-start(bf16[128,2048]{1,0:T(8,128)(2,1)S(1)} %add_convert_fusion.5), channel_id=1, source_target_pairs={{0,2},{1,3},{2,6},{3,7},{6,4},{7,5},{4,0},{5,1},{8,10},{9,11},{10,... | collective-permute-start | bytes 1572872 | tf_op jit(solution)/shard_map/ppermute | solution.py:265
  159.9 23.5 %collective-permute-start.31 = (bf16[128,2048]{1,0:T(8,128)(2,1)S(1)}, bf16[128,2048]{1,0:T(8,128)(2,1)S(1)}, u32[]{:S(2)}, u32[]{:S(2)}) collective-permute-start(bf16[128,2048]{1,0:T(8,128)(2,1)S(1)} %get-tuple-element.91), channel_id=1, source_target_pairs={{0,1},{1,0},{2,3},{3,2},{4,5},{5,4},{6,7},{7,6},{8,9},{9,8},{10,11... | collective-permute-start | bytes 1572872 | tf_op jit(solution)/shard_map/ppermute | solution.py:268
  165.4 22.2 %collective-permute-start.34 = (bf16[128,2048]{1,0:T(8,128)(2,1)S(1)}, bf16[128,2048]{1,0:T(8,128)(2,1)S(1)}, u32[]{:S(2)}, u32[]{:S(2)}) collective-permute-start(bf16[128,2048]{1,0:T(8,128)(2,1)S(1)} %add_convert_fusion.1), channel_id=1, source_target_pairs={{0,2},{1,3},{2,6},{3,7},{6,4},{7,5},{4,0},{5,1},{8,10},{9,11},{10,... | collective-permute-start | bytes 1572872 | tf_op jit(solution)/shard_map/ppermute | solution.py:265
  165.5 22.5 %collective-permute-start.18 = (bf16[128,2048]{1,0:T(8,128)(2,1)S(1)}, bf16[128,2048]{1,0:T(8,128)(2,1)S(1)}, u32[]{:S(2)}, u32[]{:S(2)}) collective-permute-start(bf16[128,2048]{1,0:T(8,128)(2,1)S(1)} %get-tuple-element.79), channel_id=1, source_target_pairs={{0,1},{1,0},{2,3},{3,2},{4,5},{5,4},{6,7},{7,6},{8,9},{9,8},{10,11... | collective-permute-start | bytes 1572872 | tf_op jit(solution)/shard_map/ppermute | solution.py:268
  176.7 22.2 %collective-permute-start.28 = (bf16[128,2048]{1,0:T(8,128)(2,1)S(1)}, bf16[128,2048]{1,0:T(8,128)(2,1)S(1)}, u32[]{:S(2)}, u32[]{:S(2)}) collective-permute-start(bf16[128,2048]{1,0:T(8,128)(2,1)S(1)} %add_convert_fusion.3), channel_id=1, source_target_pairs={{0,2},{1,3},{2,6},{3,7},{6,4},{7,5},{4,0},{5,1},{8,10},{9,11},{10,... | collective-permute-start | bytes 1572872 | tf_op jit(solution)/shard_map/ppermute | solution.py:265
  182.6 17.2 %collective-permute-start.30 = (bf16[128,2048]{1,0:T(8,128)(2,1)S(1)}, bf16[128,2048]{1,0:T(8,128)(2,1)S(1)}, u32[]{:S(2)}, u32[]{:S(2)}) collective-permute-start(bf16[128,2048]{1,0:T(8,128)(2,1)S(1)} %get-tuple-element.89), channel_id=1, source_target_pairs={{0,1},{1,0},{2,3},{3,2},{4,5},{5,4},{6,7},{7,6},{8,9},{9,8},{10,11... | collective-permute-start | bytes 1572872 | tf_op jit(solution)/shard_map/ppermute | solution.py:268
  183.5 16.4 %collective-permute-start.14 = (bf16[128,2048]{1,0:T(8,128)(2,1)S(1)}, bf16[128,2048]{1,0:T(8,128)(2,1)S(1)}, u32[]{:S(2)}, u32[]{:S(2)}) collective-permute-start(bf16[128,2048]{1,0:T(8,128)(2,1)S(1)} %get-tuple-element.76), channel_id=1, source_target_pairs={{0,1},{1,0},{2,3},{3,2},{4,5},{5,4},{6,7},{7,6},{8,9},{9,8},{10,11... | collective-permute-start | bytes 1572872 | tf_op jit(solution)/shard_map/ppermute | solution.py:268
  187.9 22.2 %collective-permute-start.35 = (bf16[128,2048]{1,0:T(8,128)(2,1)S(1)}, bf16[128,2048]{1,0:T(8,128)(2,1)S(1)}, u32[]{:S(2)}, u32[]{:S(2)}) collective-permute-start(bf16[128,2048]{1,0:T(8,128)(2,1)S(1)} %add_convert_fusion), channel_id=1, source_target_pairs={{0,2},{1,3},{2,6},{3,7},{6,4},{7,5},{4,0},{5,1},{8,10},{9,11},{10,... | collective-permute-start | bytes 1572872 | tf_op jit(solution)/shard_map/ppermute | solution.py:265
  199.1 21.5 %collective-permute-start.29 = (bf16[128,2048]{1,0:T(8,128)(2,1)S(1)}, bf16[128,2048]{1,0:T(8,128)(2,1)S(1)}, u32[]{:S(2)}, u32[]{:S(2)}) collective-permute-start(bf16[128,2048]{1,0:T(8,128)(2,1)S(1)} %add_convert_fusion.2), channel_id=1, source_target_pairs={{0,2},{1,3},{2,6},{3,7},{6,4},{7,5},{4,0},{5,1},{8,10},{9,11},{10,... | collective-permute-start | bytes 1572872 | tf_op jit(solution)/shard_map/ppermute | solution.py:265
Sparse Core Ops, SparseCore 0:
  40.3 33.1 all-gather.2

commit v2 on v1

--- a/solution.py
+++ b/solution.py
@@ -281,33 +281,34 @@
         half = weight.shape[0] // 2
         return [flip(first[:half], 2), flip(second[half:], 1)]
 
-    query_parts = [w_query] + [flip(w_query, r) for r in range(1, min(parts, 3))]
+    if parts == 4:
+        half = w_query.shape[0] // 2
+        upper, lower = w_query[:half], w_query[half:]
+        ahead = [flip(upper, 1), flip(lower, 2)]
+    else:
+        ahead = [flip(w_query, 1)]
 
     rows = enc_rows.shape[1]
     block = width // parts
-    columns = column_blocks(ids, enc_rows.reshape(rows, width), parts)
+    encoder, pairs[0] = lax.optimization_barrier((enc_rows.reshape(rows, width), pairs[0]))
+    columns = column_blocks(ids, encoder, parts)
     columns = [columns[0]] + [flip(columns[r], r) for r in range(1, parts)]
     tiles = tile_mask.shape[2]
     flags = tile_mask.reshape(1, tiles, 1).astype(jnp.bfloat16)
     flags = jnp.broadcast_to(flags, (FLAG_ROWS, tiles, block // tiles)).reshape(FLAG_ROWS, block)
     piece = jnp.concatenate(columns + [flags], axis=0)
-    piece, states, query_parts = lax.optimization_barrier((piece, states, query_parts))
+    piece, states, ahead = lax.optimization_barrier((piece, states, ahead))
     gathered = lax.all_gather(piece, "cand", axis=0)
 
     pairs.append((states, to_sib(states)))
-    for _ in range(2, chips):
-        states = to_next(states)
-        pairs.append((states, to_sib(states)))
-    if parts == 4:
-        query_parts += corner(*query_parts)
+    states = to_next(states)
+    if parts == 4:
+        query_parts = [w_query, ahead[0], flip(lower, 1), flip(upper, 2), ahead[1]]
+        query_parts += [flip(ahead[0], 2), flip(ahead[1], 1)]
     else:
-        query_parts += [flip(w_query, r) for r in range(3, parts)]
-
+        query_parts = [w_query, ahead[0]] + [flip(w_query, r) for r in range(2, parts)]
     query_parts, w_out = lax.optimization_barrier((query_parts, w_out))
     out_parts = [w_out] + [flip(w_out, r) for r in range(1, parts if parts != 4 else 3)]
-    if parts == 4:
-        out_parts += corner(*out_parts)
-    out_chunks = [out_parts[: parts // 2], out_parts[parts // 2 :]]
 
     f32, bf16 = jnp.float32, jnp.bfloat16
     elen = devices * rows
@@ -317,9 +318,13 @@
     else:
         plan = [(which, (r,), bf16 if r else f32) for which in range(2) for r in range(parts)]
     is_open, *sums = key_value(plan, gathered, w_key, w_value, parts, rows, tiles)
+    sums, out_parts, states = lax.optimization_barrier((sums, out_parts, states))
+    pairs.append((states, to_sib(states)))
+    top = to_next(states[: clen // 2])
     if parts == 4:
         (key, key_far, key_sent), (value, value_far, value_sent) = sums[:3], sums[3:]
-        came = lax.optimization_barrier((flip(key_sent, 1), flip(value_sent, 2)))
+        came = [flip(key_sent, 1), flip(value_sent, 2)]
+        came, out_parts, top = lax.optimization_barrier((came, out_parts, top))
         came = [rows_in.astype(f32) for rows_in in came]
         far = [(key_far + came[0][elen:]).astype(bf16), (value_far + came[1][elen:]).astype(bf16)]
         far = lax.optimization_barrier((flip(far[0], 2), flip(far[1], 1)))
@@ -333,28 +338,37 @@
             for r in range(1, parts):
                 own = own + flip(others[r - 1], r).astype(f32)
             projected.append(own.astype(bf16))
+    if parts == 4:
+        out_parts += corner(*out_parts)
+    out_chunks = [out_parts[: parts // 2], out_parts[parts // 2 :]]
+
+    states = jnp.concatenate([top, to_next(states[clen // 2 :])], axis=0)
+    for hop in range(3, chips):
+        pairs.append((states, to_sib(states)))
+        if hop < chips - 1:
+            states = to_next(states)
 
     steps = list(range(1, chips)) + [0]
     passed = [None] * len(out_chunks)
     queries = query(ids, *pairs[steps[0]], query_parts, parts)
     for index, step in enumerate(steps):
         context = attend(order, step, ids, queries, is_open, *projected)
-        sums = []
-        for weights in out_chunks:
+        sums, totals = [], []
+        for chunk, weights in enumerate(out_chunks):
+            if index == 1 and not chunk:
+                context, passed[0] = lax.optimization_barrier((context, passed[0]))
             mine, sib = project(context, weights)
-            sums.append((mine, to_sib(sib)))
-        if not step:
-            break
-        totals = []
-        for chunk, (mine, other) in enumerate(sums):
+            other = to_sib(sib)
+            sums.append((mine, other))
             total = mine.astype(f32) + other.astype(f32)
-            if passed[chunk] is not None:
+            if index:
                 total = total + passed[chunk].astype(f32)
             totals.append(total.astype(bf16))
-        queries = query(ids, *pairs[steps[index + 1]], query_parts, parts)
-        if not index:
-            totals, queries = lax.optimization_barrier((totals, queries))
-        passed = [to_next(total) for total in totals]
+            if not index and not chunk:
+                context, totals[0] = lax.optimization_barrier((context, totals[0]))
+        if step:
+            passed = [to_next(total) for total in totals]
+            queries = query(ids, *pairs[steps[index + 1]], query_parts, parts)
     last = [part for (mine, other), came in zip(sums, passed) for part in (mine, other, came)]
     return finish(ids, counts, last, parts, width).reshape(cand_states.shape)
 

time: 230 us -> 216 us (0.939)
  waiting for transfers between devices: 144 us -> 117 us
  starting transfers between devices: 28.9 us -> 37.5 us
  local copies, waits for them, and re-layouts: 3.87 us -> 11.1 us
    ppermute x9 -> x10, waiting for transfers between devices: 64 us -> 50.9 us  [to_next(): return lax.ppermute(value, 'cand', along)]
    ppermute x9 -> x10, starting transfers between devices: 6.86 us -> 16 us  [to_next(): return lax.ppermute(value, 'cand', along)]
    all_gather x1, waiting for transfers between devices: 28.3 us -> 20.2 us  [shards(): gathered = lax.all_gather(piece, 'cand', axis=0)]
    ppermute x15 -> x17, waiting for transfers between devices: 51.5 us -> 45.5 us  [flip(): return lax.ppermute(value, 'prod', [(q, q ^ r) for q in range(parts)])]
    unnamed x28 -> x55, local copies, waits for them, and re-layouts: 2.13 us -> 7.5 us
    slice x0 -> x2, local copies, waits for them, and re-layouts: none -> 3.51 us  [the longest x1 2.22 us: shards(): upper, lower = (w_query[:half], w_query[half:])]
    ppermute x15 -> x17, starting transfers between devices: 19.4 us -> 19.1 us  [flip(): return lax.ppermute(value, 'prod', [(q, q ^ r) for q in range(parts)])]
  transfers between devices with their start and end apart: 37 -> 40, of which waited for: 17 -> 21; matrix products, arithmetic and copies ran while one was open for 2% -> 3% of each run, Pallas kernels for 14% -> 14%
where the time goes in v2:
time: 216 us
  waiting for transfers between devices  117 us (54%)
  starting transfers between devices  37.5 us (17%)
  Pallas kernels  33.2 us (15%)
  between operations  14.6 us (7%)
  local copies, waits for them, and re-layouts  11.1 us (5%)
  other arithmetic  2.7 us (1%)
    ppermute x10, waiting for transfers between devices, to_next(): return lax.ppermute(value, 'cand', along)  50.9 us
    ppermute x17, waiting for transfers between devices, flip(): return lax.ppermute(value, 'prod', [(q, q ^ r) for q in range(parts)])  45.5 us
    all_gather x1, waiting for transfers between devices, shards(): gathered = lax.all_gather(piece, 'cand', axis=0)  20.2 us
    ppermute x17, starting transfers between devices, flip(): return lax.ppermute(value, 'prod', [(q, q ^ r) for q in range(parts)])  19.1 us
    ppermute x10, starting transfers between devices, to_next(): return lax.ppermute(value, 'cand', along)  16 us
    pallas_call x4, Pallas kernels, query(): pl.pallas_call(functools.partial(query_kernel, len(weights), parts), out_...  10.3 us
    pallas_call x4, Pallas kernels, attend(): pl.pallas_call(functools.partial(attend_kernel, order, step), out_shape=j...  9 us
    unnamed x55, local copies, waits for them, and re-layouts  7.5 us
  transfers between devices with their start and end apart: 40, of which 21 were waited for; matrix products, arithmetic and copies ran while one was open for 3% of the time, Pallas kernels for 14%

profile of v2, /device:TPU:0, one launch (start us, length us, event | category | flops | bytes accessed | tf_op | source)
XLA Modules:
  0.0 215.8 jit_solution(4871362478657662018)
XLA Ops:
  7.0 2.6 %collective-permute-start.4 = (bf16[128,4096]{1,0:T(8,128)(2,1)}, bf16[128,4096]{1,0:T(8,128)(2,1)}, u32[]{:S(2)}, u32[]{:S(2)}) collective-permute-start(bf16[128,4096]{1,0:T(8,128)(2,1)} %bitcast.12), channel_id=1, source_target_pairs={{0,2},{1,3},{2,6},{3,7},{6,4},{7,5},{4,0},{5,1},{8,10},{9,11},{10,... | collective-permute-start | bytes 3145736 | tf_op jit(solution)/shard_map/ppermute | solution.py:265
  9.6 2.2 %fusion.7 = (bf16[512,512]{1,0:T(8,128)(2,1)}, bf16[512,512]{1,0:T(8,128)(2,1)}) fusion(bf16[1024,512]{1,0:T(8,128)(2,1)} %refs_0_.5), kind=kLoop, calls=%fused_computation.27 | loop fusion | bytes 2097152 | tf_op jit(solution)/shard_map/slice | solution.py:286
  11.8 1.5 collective-permute-start.5
  13.3 1.5 collective-permute-start.6
  15.6 1.0 copy-done.15
  16.6 0.9 copy-done.17
  19.2 8.2 %collective-permute-done.1 = bf16[32,1024]{1,0:T(8,128)(2,1)S(1)} collective-permute-done((bf16[32,1024]{1,0:T(8,128)(2,1)S(1)}, bf16[32,1024]{1,0:T(8,128)(2,1)S(1)}, u32[]{:S(2)}, u32[]{:S(2)}) %collective-permute-start.1) | collective-permute-done | bytes 65568 | tf_op jit(solution)/shard_map/ppermute | solution.py:271
  27.5 2.4 %collective-permute-start.3 = (bf16[32,1024]{1,0:T(8,128)(2,1)S(1)}, bf16[32,1024]{1,0:T(8,128)(2,1)S(1)}, u32[]{:S(2)}, u32[]{:S(2)}) collective-permute-start(bf16[32,1024]{1,0:T(8,128)(2,1)S(1)} %get-tuple-element.75), channel_id=1, source_target_pairs={{0,24},{8,16},{16,8},{24,0},{1,25},{9,17},{17,9},{25,1},{2,26},{10... | collective-permute-start | bytes 196616 | tf_op jit(solution)/shard_map/ppermute | solution.py:271
  29.9 2.7 %collective-permute-done.3 = bf16[32,1024]{1,0:T(8,128)(2,1)S(1)} collective-permute-done((bf16[32,1024]{1,0:T(8,128)(2,1)S(1)}, bf16[32,1024]{1,0:T(8,128)(2,1)S(1)}, u32[]{:S(2)}, u32[]{:S(2)}) %collective-permute-start.3) | collective-permute-done | bytes 65568 | tf_op jit(solution)/shard_map/ppermute | solution.py:271
  32.7 2.0 collective-permute-done.4.mine
  34.8 1.6 collective-permute-start.7
  36.4 1.5 collective-permute-start.8
  38.4 0.8 copy-done.2
  39.7 0.8 copy-done.4
  40.5 1.2 collective-permute-start.13
  41.7 8.1 %collective-permute-done.7.refs_2_ = bf16[512,512]{1,0:T(8,128)(2,1)S(1)} collective-permute-done((bf16[512,512]{1,0:T(8,128)(2,1)}, bf16[512,512]{1,0:T(8,128)(2,1)S(1)}, u32[]{:S(2)}, u32[]{:S(2)}) %collective-permute-start.7) | collective-permute-done | bytes 524320 | tf_op jit(solution)/shard_map/ppermute | solution.py:271
  49.8 0.8 copy-done.6
  50.6 0.8 collective-permute-done.8.refs_3_
  51.4 0.8 copy-done.8
  52.2 8.9 %collective-permute-done.9.refs_5_ = bf16[512,512]{1,0:T(8,128)(2,1)S(1)} collective-permute-done((bf16[512,512]{1,0:T(8,128)(2,1)S(1)}, bf16[512,512]{1,0:T(8,128)(2,1)S(1)}, u32[]{:S(2)}, u32[]{:S(2)}) %collective-permute-start.9) | collective-permute-done | bytes 524320 | tf_op jit(solution)/shard_map/ppermute | solution.py:271
  61.1 0.8 copy-done.10
  61.9 0.9 copy-done.12
  63.4 1.4 collective-permute-start.12
  64.8 20.2 %all-gather.3.cloned.1.call-done = bf16[1152,1024]{1,0:T(8,128)(2,1)} async-done(((bf16[144,1024]{1,0:T(8,128)(2,1)}), bf16[1152,1024]{1,0:T(8,128)(2,1)}) %all-gather.3.cloned.1.call-update) | async-done | bytes 2359312 | tf_op jit(solution)/shard_map/all_gather | solution.py:301
  85.1 5.7 %key_value.1 = (f32[8,256]{1,0:T(8,128)}, f32[256,512]{1,0:T(8,128)}, f32[256,512]{1,0:T(8,128)}, bf16[512,512]{1,0:T(8,128)(2,1)}, f32[256,512]{1,0:T(8,128)}, ...) custom-call(bf16[8,144,1024]{2,1,0:T(8,128)(2,1)} %bitcast.15, bf16[1024,512]{1,0:T(8,128)(2,1)} %w_key.1, ...), custom_call_target="tpu_custom_call" | custom-call | flops 1 | bytes 1 | tf_op jit(solution)/shard_map/key_value/pallas_call | solution.py:76
  90.8 1.5 collective-permute-start.14
  92.3 1.5 collective-permute-start.15
  93.8 1.3 fusion.6
  95.8 9.4 %collective-permute-done.14 = bf16[512,512]{1,0:T(8,128)(2,1)S(1)} collective-permute-done((bf16[512,512]{1,0:T(8,128)(2,1)}, bf16[512,512]{1,0:T(8,128)(2,1)S(1)}, u32[]{:S(2)}, u32[]{:S(2)}) %collective-permute-start.14) | collective-permute-done | bytes 524320 | tf_op jit(solution)/shard_map/ppermute | solution.py:271
  105.1 1.2 collective-permute-done.15
  106.4 3.3 %collective-permute-done.16 = bf16[64,4096]{1,0:T(8,128)(2,1)S(1)} collective-permute-done((bf16[64,4096]{1,0:T(8,128)(2,1)S(1)}, bf16[64,4096]{1,0:T(8,128)(2,1)S(1)}, u32[]{:S(2)}, u32[]{:S(2)}) %collective-permute-start.16) | collective-permute-done | bytes 524320 | tf_op jit(solution)/shard_map/ppermute | solution.py:265
  111.9 2.9 %query.7.query_ref = bf16[256,512]{1,0:T(8,128)(2,1)S(1)} custom-call(s32[2]{0:T(128)S(1)} %pad_add_fusion.ids, bf16[128,4096]{1,0:T(8,128)(2,1)} %collective-permute-done.4.mine, bf16[128,4096]{1,0:T(8,128)(2,1)S(1)} %collective-permute-done.24.sib, bf16[1024,512]{1,0:T(8,128)(2,1)S(1)} %copy-done, bf16[512,512]{1,0:T(8,128)(2,1)S(1)} %copy-done.3, ...), custom_call_target="tpu_custom_call" | custom-call | flops 1 | bytes 1 | tf_op jit(solution)/shard_map/query/pallas_call | solution.py:116
  114.9 1.3 collective-permute-start.20
  116.2 0.9 collective-permute-done.17
  117.9 2.3 %attend.7.context_ref = bf16[256,512]{1,0:T(8,128)(2,1)S(1)} custom-call(s32[2]{0:T(128)S(1)} %pad_add_fusion.ids, bf16[256,512]{1,0:T(8,128)(2,1)S(1)} %query.7.query_ref, f32[8,256]{1,0:T(8,128)S(1)} %copy-done.18, bf16[256,512]{1,0:T(8,128)(2,1)S(1)} %get-tuple-element.138.key_ref, bf16[256,512]{1,0:T(8,128)(2,1)S(1)} %get-tuple-element.137.value_ref), custom_call_target="tpu_custom_call" | custom-call | flops 1 | bytes 1 | tf_op jit(solution)/shard_map/attend/pallas_call | solution.py:175
  120.2 0.7 project.10
  121.1 1.5 collective-permute-start.30
  123.2 6.9 %collective-permute-done.20 = bf16[64,4096]{1,0:T(8,128)(2,1)S(1)} collective-permute-done((bf16[64,4096]{1,0:T(8,128)(2,1)S(1)}, bf16[64,4096]{1,0:T(8,128)(2,1)S(1)}, u32[]{:S(2)}, u32[]{:S(2)}) %collective-permute-start.20) | collective-permute-done | bytes 524320 | tf_op jit(solution)/shard_map/ppermute | solution.py:265
  130.4 1.5 collective-permute-start.26
  131.9 3.6 %collective-permute-done.30.refs_1_ = bf16[256,1024]{1,0:T(8,128)(2,1)S(1)} collective-permute-done((bf16[256,1024]{1,0:T(8,128)(2,1)S(1)}, bf16[256,1024]{1,0:T(8,128)(2,1)S(1)}, u32[]{:S(2)}, u32[]{:S(2)}) %collective-permute-start.30) | collective-permute-done | bytes 524320 | tf_op jit(solution)/shard_map/ppermute | solution.py:271
  135.4 1.3 collective-permute-done.31.refs_2_
  136.7 0.7 project.15
  137.6 2.9 %query.6.query_ref = bf16[256,512]{1,0:T(8,128)(2,1)S(1)} custom-call(s32[2]{0:T(128)S(1)} %pad_add_fusion.ids, bf16[128,4096]{1,0:T(8,128)(2,1)} %collective-permute-done.13.mine, bf16[128,4096]{1,0:T(8,128)(2,1)S(1)} %collective-permute-done.23.sib, bf16[1024,512]{1,0:T(8,128)(2,1)S(1)} %copy-done, bf16[512,512]{1,0:T(8,128)(2,1)S(1)} %copy-done.3, ...), custom_call_target="tpu_custom_call" | custom-call | flops 1 | bytes 1 | tf_op jit(solution)/shard_map/query/pallas_call | solution.py:116
  140.5 2.3 %attend.6.context_ref = bf16[256,512]{1,0:T(8,128)(2,1)S(1)} custom-call(s32[2]{0:T(128)S(1)} %pad_add_fusion.ids, bf16[256,512]{1,0:T(8,128)(2,1)S(1)} %query.6.query_ref, f32[8,256]{1,0:T(8,128)S(1)} %copy-done.18, bf16[256,512]{1,0:T(8,128)(2,1)S(1)} %get-tuple-element.138.key_ref, bf16[256,512]{1,0:T(8,128)(2,1)S(1)} %get-tuple-element.137.value_ref), custom_call_target="tpu_custom_call" | custom-call | flops 1 | bytes 1 | tf_op jit(solution)/shard_map/attend/pallas_call | solution.py:175
  142.7 3.1 %collective-permute-done.26 = bf16[128,2048]{1,0:T(8,128)(2,1)S(1)} collective-permute-done((bf16[128,2048]{1,0:T(8,128)(2,1)S(1)}, bf16[128,2048]{1,0:T(8,128)(2,1)S(1)}, u32[]{:S(2)}, u32[]{:S(2)}) %collective-permute-start.26) | collective-permute-done | bytes 524320 | tf_op jit(solution)/shard_map/ppermute | solution.py:265
  146.8 1.3 collective-permute-start.36
  148.1 0.7 project.14
  149.1 2.2 %query.5.query_ref = bf16[256,512]{1,0:T(8,128)(2,1)S(1)} custom-call(s32[2]{0:T(128)S(1)} %pad_add_fusion.ids, bf16[128,4096]{1,0:T(8,128)(2,1)S(1)} %constant_dynamic-update-slice_fusion.5.mine, bf16[128,4096]{1,0:T(8,128)(2,1)S(1)} %collective-permute-done.21.sib, bf16[1024,512]{1,0:T(8,128)(2,1)S(1)} %copy-done, bf16[512,512]{1,0:T(8,128)(2,1)S(1)} %copy-done.3, ...), custom_call_target="tpu_custom_call" | custom-call | flops 1 | bytes 1 | tf_op jit(solution)/shard_map/query/pallas_call | solution.py:116
  151.3 2.2 %attend.5.context_ref = bf16[256,512]{1,0:T(8,128)(2,1)S(1)} custom-call(s32[2]{0:T(128)S(1)} %pad_add_fusion.ids, bf16[256,512]{1,0:T(8,128)(2,1)S(1)} %query.5.query_ref, f32[8,256]{1,0:T(8,128)S(1)} %copy-done.18, bf16[256,512]{1,0:T(8,128)(2,1)S(1)} %get-tuple-element.138.key_ref, bf16[256,512]{1,0:T(8,128)(2,1)S(1)} %get-tuple-element.137.value_ref), custom_call_target="tpu_custom_call" | custom-call | flops 1 | bytes 1 | tf_op jit(solution)/shard_map/attend/pallas_call | solution.py:175
  154.6 0.7 project.13
  155.9 3.4 %collective-permute-start.28 = (bf16[128,2048]{1,0:T(8,128)(2,1)S(1)}, bf16[128,2048]{1,0:T(8,128)(2,1)S(1)}, u32[]{:S(2)}, u32[]{:S(2)}) collective-permute-start(bf16[128,2048]{1,0:T(8,128)(2,1)S(1)} %add_convert_fusion.4), channel_id=1, source_target_pairs={{0,2},{1,3},{2,6},{3,7},{6,4},{7,5},{4,0},{5,1},{8,10},{9,11},{10,... | collective-permute-start | bytes 1572872 | tf_op jit(solution)/shard_map/ppermute | solution.py:265
  159.3 3.1 %collective-permute-done.36 = bf16[128,2048]{1,0:T(8,128)(2,1)S(1)} collective-permute-done((bf16[128,2048]{1,0:T(8,128)(2,1)S(1)}, bf16[128,2048]{1,0:T(8,128)(2,1)S(1)}, u32[]{:S(2)}, u32[]{:S(2)}) %collective-permute-start.36) | collective-permute-done | bytes 524320 | tf_op jit(solution)/shard_map/ppermute | solution.py:265
  162.7 1.5 collective-permute-start.37
  164.2 2.2 %query.4.query_ref = bf16[256,512]{1,0:T(8,128)(2,1)S(1)} custom-call(s32[2]{0:T(128)S(1)} %pad_add_fusion.ids, bf16[128,4096]{1,0:T(8,128)(2,1)S(1)} %bitcast.13, bf16[128,4096]{1,0:T(8,128)(2,1)S(1)} %copy-done.16, bf16[1024,512]{1,0:T(8,128)(2,1)S(1)} %copy-done, bf16[512,512]{1,0:T(8,128)(2,1)S(1)} %copy-done.3, bf16[512,512]{1,0:T(8,128)(2,1)S(1)} %copy-done.7, ...), custom_call_target="tpu_custom_call" | custom-call | flops 1 | bytes 1 | tf_op jit(solution)/shard_map/query/pallas_call | solution.py:116
  166.4 2.2 %attend.4.context_ref = bf16[256,512]{1,0:T(8,128)(2,1)S(1)} custom-call(s32[2]{0:T(128)S(1)} %pad_add_fusion.ids, bf16[256,512]{1,0:T(8,128)(2,1)S(1)} %query.4.query_ref, f32[8,256]{1,0:T(8,128)S(1)} %copy-done.18, bf16[256,512]{1,0:T(8,128)(2,1)S(1)} %get-tuple-element.138.key_ref, bf16[256,512]{1,0:T(8,128)(2,1)S(1)} %get-tuple-element.137.value_ref), custom_call_target="tpu_custom_call" | custom-call | flops 1 | bytes 1 | tf_op jit(solution)/shard_map/attend/pallas_call | solution.py:175
  168.7 0.7 project.8
  169.5 0.7 project.12
  170.8 2.9 %collective-permute-done.28 = bf16[128,2048]{1,0:T(8,128)(2,1)S(1)} collective-permute-done((bf16[128,2048]{1,0:T(8,128)(2,1)S(1)}, bf16[128,2048]{1,0:T(8,128)(2,1)S(1)}, u32[]{:S(2)}, u32[]{:S(2)}) %collective-permute-start.28) | collective-permute-done | bytes 524320 | tf_op jit(solution)/shard_map/ppermute | solution.py:265
  173.9 1.3 collective-permute-start.29
  175.2 9.7 %collective-permute-done.37 = bf16[128,2048]{1,0:T(8,128)(2,1)S(1)} collective-permute-done((bf16[128,2048]{1,0:T(8,128)(2,1)S(1)}, bf16[128,2048]{1,0:T(8,128)(2,1)S(1)}, u32[]{:S(2)}, u32[]{:S(2)}) %collective-permute-start.37) | collective-permute-done | bytes 524320 | tf_op jit(solution)/shard_map/ppermute | solution.py:265
  185.2 1.3 collective-permute-start.38
  187.1 9.0 %collective-permute-done.29.refs_2_ = bf16[128,2048]{1,0:T(8,128)(2,1)S(1)} collective-permute-done((bf16[128,2048]{1,0:T(8,128)(2,1)S(1)}, bf16[128,2048]{1,0:T(8,128)(2,1)S(1)}, u32[]{:S(2)}, u32[]{:S(2)}) %collective-permute-start.29) | collective-permute-done | bytes 524320 | tf_op jit(solution)/shard_map/ppermute | solution.py:265
  196.2 10.8 %collective-permute-done.38.refs_5_ = bf16[128,2048]{1,0:T(8,128)(2,1)S(1)} collective-permute-done((bf16[128,2048]{1,0:T(8,128)(2,1)S(1)}, bf16[128,2048]{1,0:T(8,128)(2,1)S(1)}, u32[]{:S(2)}, u32[]{:S(2)}) %collective-permute-start.38) | collective-permute-done | bytes 524320 | tf_op jit(solution)/shard_map/ppermute | solution.py:265
  207.0 2.0 finish.1
  (110 shorter events, 13.6 us)
Async XLA Ops:
  6.5 56.2 %copy-start.1 = (bf16[512,1024]{1,0:T(8,128)(2,1)S(1)}, bf16[512,1024]{1,0:T(8,128)(2,1)}, u32[]{:S(2)}) copy-start(bf16[512,1024]{1,0:T(8,128)(2,1)} %refs_0_.7) | copy-start | bytes 3145732
  6.5 78.5 %all-gather.3.cloned.1.call-start = ((), (), s32[]{:S(2)}) async-start(), calls=%async_computation | async-start | bytes 2654208 | tf_op jit(solution)/shard_map/all_gather | solution.py:301
  6.5 9.1 %collective-permute-start = (bf16[128,4096]{1,0:T(8,128)(2,1)}, bf16[128,4096]{1,0:T(8,128)(2,1)S(1)}, u32[]{:S(2)}, u32[]{:S(2)}) collective-permute-start(bf16[128,4096]{1,0:T(8,128)(2,1)} %bitcast.11), channel_id=1, source_target_pairs={{0,1},{1,0},{2,3},{3,2},{4,5},{5,4},{6,7},{7,6},{8,9},{9,8},{10,11... | collective-permute-start | bytes 3145736 | tf_op jit(solution)/shard_map/ppermute | solution.py:268
  7.0 27.7 %collective-permute-start.4 = (bf16[128,4096]{1,0:T(8,128)(2,1)}, bf16[128,4096]{1,0:T(8,128)(2,1)}, u32[]{:S(2)}, u32[]{:S(2)}) collective-permute-start(bf16[128,4096]{1,0:T(8,128)(2,1)} %bitcast.12), channel_id=1, source_target_pairs={{0,2},{1,3},{2,6},{3,7},{6,4},{7,5},{4,0},{5,1},{8,10},{9,11},{10,... | collective-permute-start | bytes 3145736 | tf_op jit(solution)/shard_map/ppermute | solution.py:265
  11.8 20.9 %collective-permute-start.5 = (bf16[512,512]{1,0:T(8,128)(2,1)}, bf16[512,512]{1,0:T(8,128)(2,1)S(1)}, u32[]{:S(2)}, u32[]{:S(2)}) collective-permute-start(bf16[512,512]{1,0:T(8,128)(2,1)} %get-tuple-element.136), channel_id=1, source_target_pairs={{0,8},{8,0},{16,24},{24,16},{1,9},{9,1},{17,25},{25,17},{2,10},{10... | collective-permute-start | bytes 1572872 | tf_op jit(solution)/shard_map/ppermute | solution.py:271
  13.3 19.4 %collective-permute-start.6 = (bf16[512,512]{1,0:T(8,128)(2,1)}, bf16[512,512]{1,0:T(8,128)(2,1)S(1)}, u32[]{:S(2)}, u32[]{:S(2)}) collective-permute-start(bf16[512,512]{1,0:T(8,128)(2,1)} %get-tuple-element.135), channel_id=1, source_target_pairs={{0,16},{8,24},{16,0},{24,8},{1,17},{9,25},{17,1},{25,9},{2,18},{10... | collective-permute-start | bytes 1572872 | tf_op jit(solution)/shard_map/ppermute | solution.py:271
  15.6 1.0 copy-start.15
  16.6 0.9 copy-start.17
  18.1 9.3 %collective-permute-start.1 = (bf16[32,1024]{1,0:T(8,128)(2,1)S(1)}, bf16[32,1024]{1,0:T(8,128)(2,1)S(1)}, u32[]{:S(2)}, u32[]{:S(2)}) collective-permute-start(bf16[32,1024]{1,0:T(8,128)(2,1)S(1)} %get-tuple-element.73), channel_id=1, source_target_pairs={{0,8},{8,0},{16,24},{24,16},{1,9},{9,1},{17,25},{25,17},{2,10},{10... | collective-permute-start | bytes 196616 | tf_op jit(solution)/shard_map/ppermute | solution.py:271
  18.7 11.2 %collective-permute-start.2 = (bf16[32,1024]{1,0:T(8,128)(2,1)S(1)}, bf16[32,1024]{1,0:T(8,128)(2,1)S(1)}, u32[]{:S(2)}, u32[]{:S(2)}) collective-permute-start(bf16[32,1024]{1,0:T(8,128)(2,1)S(1)} %get-tuple-element.74), channel_id=1, source_target_pairs={{0,16},{8,24},{16,0},{24,8},{1,17},{9,25},{17,1},{25,9},{2,18},{10... | collective-permute-start | bytes 196616 | tf_op jit(solution)/shard_map/ppermute | solution.py:271
  27.5 5.2 %collective-permute-start.3 = (bf16[32,1024]{1,0:T(8,128)(2,1)S(1)}, bf16[32,1024]{1,0:T(8,128)(2,1)S(1)}, u32[]{:S(2)}, u32[]{:S(2)}) collective-permute-start(bf16[32,1024]{1,0:T(8,128)(2,1)S(1)} %get-tuple-element.75), channel_id=1, source_target_pairs={{0,24},{8,16},{16,8},{24,0},{1,25},{9,17},{17,9},{25,1},{2,26},{10... | collective-permute-start | bytes 196616 | tf_op jit(solution)/shard_map/ppermute | solution.py:271
  32.6 2.1 copy-start.23
  34.8 15.1 %collective-permute-start.7 = (bf16[512,512]{1,0:T(8,128)(2,1)}, bf16[512,512]{1,0:T(8,128)(2,1)S(1)}, u32[]{:S(2)}, u32[]{:S(2)}) collective-permute-start(bf16[512,512]{1,0:T(8,128)(2,1)} %get-tuple-element.135), channel_id=1, source_target_pairs={{0,8},{8,0},{16,24},{24,16},{1,9},{9,1},{17,25},{25,17},{2,10},{10... | collective-permute-start | bytes 1572872 | tf_op jit(solution)/shard_map/ppermute | solution.py:271
  36.4 15.1 %collective-permute-start.8 = (bf16[512,512]{1,0:T(8,128)(2,1)}, bf16[512,512]{1,0:T(8,128)(2,1)S(1)}, u32[]{:S(2)}, u32[]{:S(2)}) collective-permute-start(bf16[512,512]{1,0:T(8,128)(2,1)} %get-tuple-element.136), channel_id=1, source_target_pairs={{0,16},{8,24},{16,0},{24,8},{1,17},{9,25},{17,1},{25,9},{2,18},{10... | collective-permute-start | bytes 1572872 | tf_op jit(solution)/shard_map/ppermute | solution.py:271
  37.9 23.2 %collective-permute-start.9 = (bf16[512,512]{1,0:T(8,128)(2,1)S(1)}, bf16[512,512]{1,0:T(8,128)(2,1)S(1)}, u32[]{:S(2)}, u32[]{:S(2)}) collective-permute-start(bf16[512,512]{1,0:T(8,128)(2,1)S(1)} %collective-permute-done.5.refs_1_), channel_id=1, source_target_pairs={{0,16},{8,24},{16,0},{24,8},{1,17},{9,25},{17,1},{25,9},{2,18},{10... | collective-permute-start | bytes 1572872 | tf_op jit(solution)/shard_map/ppermute | solution.py:271
  38.4 0.8 copy-start.2
  39.2 22.7 %collective-permute-start.10 = (bf16[512,512]{1,0:T(8,128)(2,1)S(1)}, bf16[512,512]{1,0:T(8,128)(2,1)S(1)}, u32[]{:S(2)}, u32[]{:S(2)}) collective-permute-start(bf16[512,512]{1,0:T(8,128)(2,1)S(1)} %collective-permute-done.6.refs_4_), channel_id=1, source_target_pairs={{0,8},{8,0},{16,24},{24,16},{1,9},{9,1},{17,25},{25,17},{2,10},{10... | collective-permute-start | bytes 1572872 | tf_op jit(solution)/shard_map/ppermute | solution.py:271
  39.7 0.8 copy-start.4
  40.5 50.3 %collective-permute-start.13 = (bf16[128,4096]{1,0:T(8,128)(2,1)}, bf16[128,4096]{1,0:T(8,128)(2,1)}, u32[]{:S(2)}, u32[]{:S(2)}) collective-permute-start(bf16[128,4096]{1,0:T(8,128)(2,1)} %collective-permute-done.4.mine), channel_id=1, source_target_pairs={{0,2},{1,3},{2,6},{3,7},{6,4},{7,5},{4,0},{5,1},{8,10},{9,11},{10,... | collective-permute-start | bytes 3145736 | tf_op jit(solution)/shard_map/ppermute | solution.py:265
  49.8 0.8 copy-start.6
  51.4 0.8 copy-start.8
  61.1 0.8 copy-start.10
  61.9 0.9 copy-start.12
  62.8 28.0 %collective-permute-start.11 = (bf16[512,1024]{1,0:T(8,128)(2,1)S(1)}, bf16[512,1024]{1,0:T(8,128)(2,1)S(1)}, u32[]{:S(2)}, u32[]{:S(2)}) collective-permute-start(bf16[512,1024]{1,0:T(8,128)(2,1)S(1)} %copy-done.1), channel_id=1, source_target_pairs={{0,8},{8,0},{16,24},{24,16},{1,9},{9,1},{17,25},{25,17},{2,10},{10... | collective-permute-start | bytes 3145736 | tf_op jit(solution)/shard_map/ppermute | solution.py:271
  63.4 27.3 %collective-permute-start.12 = (bf16[512,1024]{1,0:T(8,128)(2,1)S(1)}, bf16[512,1024]{1,0:T(8,128)(2,1)S(1)}, u32[]{:S(2)}, u32[]{:S(2)}) collective-permute-start(bf16[512,1024]{1,0:T(8,128)(2,1)S(1)} %copy-done.1), channel_id=1, source_target_pairs={{0,16},{8,24},{16,0},{24,8},{1,17},{9,25},{17,1},{25,9},{2,18},{10... | collective-permute-start | bytes 3145736 | tf_op jit(solution)/shard_map/ppermute | solution.py:271
  90.8 19.2 %copy-start.20 = (f32[256,512]{1,0:T(8,128)S(1)}, f32[256,512]{1,0:T(8,128)}, u32[]{:S(2)}) copy-start(f32[256,512]{1,0:T(8,128)} %get-tuple-element.103) | copy-start | bytes 1572868
  90.8 14.4 %collective-permute-start.14 = (bf16[512,512]{1,0:T(8,128)(2,1)}, bf16[512,512]{1,0:T(8,128)(2,1)S(1)}, u32[]{:S(2)}, u32[]{:S(2)}) collective-permute-start(bf16[512,512]{1,0:T(8,128)(2,1)} %get-tuple-element.96), channel_id=1, source_target_pairs={{0,8},{8,0},{16,24},{24,16},{1,9},{9,1},{17,25},{25,17},{2,10},{10... | collective-permute-start | bytes 1572872 | tf_op jit(solution)/shard_map/ppermute | solution.py:271
  92.3 14.0 %collective-permute-start.15 = (bf16[512,512]{1,0:T(8,128)(2,1)}, bf16[512,512]{1,0:T(8,128)(2,1)S(1)}, u32[]{:S(2)}, u32[]{:S(2)}) collective-permute-start(bf16[512,512]{1,0:T(8,128)(2,1)} %get-tuple-element.97), channel_id=1, source_target_pairs={{0,16},{8,24},{16,0},{24,8},{1,17},{9,25},{17,1},{25,9},{2,18},{10... | collective-permute-start | bytes 1572872 | tf_op jit(solution)/shard_map/ppermute | solution.py:271
  95.1 15.5 %copy-start.19 = (f32[256,512]{1,0:T(8,128)S(1)}, f32[256,512]{1,0:T(8,128)}, u32[]{:S(2)}) copy-start(f32[256,512]{1,0:T(8,128)} %get-tuple-element.104) | copy-start | bytes 1572868
  95.1 14.5 %collective-permute-start.16 = (bf16[64,4096]{1,0:T(8,128)(2,1)S(1)}, bf16[64,4096]{1,0:T(8,128)(2,1)S(1)}, u32[]{:S(2)}, u32[]{:S(2)}) collective-permute-start(bf16[64,4096]{1,0:T(8,128)(2,1)S(1)} %get-tuple-element.134), channel_id=1, source_target_pairs={{0,2},{1,3},{2,6},{3,7},{6,4},{7,5},{4,0},{5,1},{8,10},{9,11},{10,... | collective-permute-start | bytes 1572872 | tf_op jit(solution)/shard_map/ppermute | solution.py:265
  95.8 15.6 %collective-permute-start.24 = (bf16[128,4096]{1,0:T(8,128)(2,1)}, bf16[128,4096]{1,0:T(8,128)(2,1)S(1)}, u32[]{:S(2)}, u32[]{:S(2)}) collective-permute-start(bf16[128,4096]{1,0:T(8,128)(2,1)} %collective-permute-done.4.mine), channel_id=1, source_target_pairs={{0,1},{1,0},{2,3},{3,2},{4,5},{5,4},{6,7},{7,6},{8,9},{9,8},{10,11... | collective-permute-start | bytes 3145736 | tf_op jit(solution)/shard_map/ppermute | solution.py:268
  109.7 1.6 copy-start
  109.8 1.6 copy-start.3
  109.8 1.6 copy-start.5
  109.8 1.6 copy-start.7
  109.8 1.8 copy-start.9
  109.8 1.9 copy-start.11
  109.8 2.1 copy-start.13
  110.1 7.1 %collective-permute-start.17 = (bf16[256,512]{1,0:T(8,128)(2,1)S(1)}, bf16[256,512]{1,0:T(8,128)(2,1)S(1)}, u32[]{:S(2)}, u32[]{:S(2)}) collective-permute-start(bf16[256,512]{1,0:T(8,128)(2,1)S(1)} %fusion.3), channel_id=1, source_target_pairs={{0,16},{8,24},{16,0},{24,8},{1,17},{9,25},{17,1},{25,9},{2,18},{10... | collective-permute-start | bytes 786440 | tf_op jit(solution)/shard_map/ppermute | solution.py:271
  110.8 6.8 %copy-start.21 = (f32[256,512]{1,0:T(8,128)S(1)}, f32[256,512]{1,0:T(8,128)}, u32[]{:S(2)}) copy-start(f32[256,512]{1,0:T(8,128)} %get-tuple-element.95) | copy-start | bytes 1572868
  110.8 6.8 %copy-start.22 = (f32[256,512]{1,0:T(8,128)S(1)}, f32[256,512]{1,0:T(8,128)}, u32[]{:S(2)}) copy-start(f32[256,512]{1,0:T(8,128)} %get-tuple-element.107) | copy-start | bytes 1572868
  110.8 6.8 %collective-permute-start.18 = (bf16[256,512]{1,0:T(8,128)(2,1)S(1)}, bf16[256,512]{1,0:T(8,128)(2,1)S(1)}, u32[]{:S(2)}, u32[]{:S(2)}) collective-permute-start(bf16[256,512]{1,0:T(8,128)(2,1)S(1)} %fusion.2), channel_id=1, source_target_pairs={{0,8},{8,0},{16,24},{24,16},{1,9},{9,1},{17,25},{25,17},{2,10},{10... | collective-permute-start | bytes 786440 | tf_op jit(solution)/shard_map/ppermute | solution.py:271
  114.8 3.1 %copy-start.18 = (f32[8,256]{1,0:T(8,128)S(1)}, f32[8,256]{1,0:T(8,128)}, u32[]{:S(2)}) copy-start(f32[8,256]{1,0:T(8,128)} %get-tuple-element.86.open_ref) | copy-start | bytes 24580
  114.8 22.7 %collective-permute-start.23 = (bf16[128,4096]{1,0:T(8,128)(2,1)}, bf16[128,4096]{1,0:T(8,128)(2,1)S(1)}, u32[]{:S(2)}, u32[]{:S(2)}) collective-permute-start(bf16[128,4096]{1,0:T(8,128)(2,1)} %collective-permute-done.13.mine), channel_id=1, source_target_pairs={{0,1},{1,0},{2,3},{3,2},{4,5},{5,4},{6,7},{7,6},{8,9},{9,8},{10,11... | collective-permute-start | bytes 3145736 | tf_op jit(solution)/shard_map/ppermute | solution.py:268
  114.9 15.2 %collective-permute-start.20 = (bf16[64,4096]{1,0:T(8,128)(2,1)S(1)}, bf16[64,4096]{1,0:T(8,128)(2,1)S(1)}, u32[]{:S(2)}, u32[]{:S(2)}) collective-permute-start(bf16[64,4096]{1,0:T(8,128)(2,1)S(1)} %get-tuple-element.133), channel_id=1, source_target_pairs={{0,2},{1,3},{2,6},{3,7},{6,4},{7,5},{4,0},{5,1},{8,10},{9,11},{10,... | collective-permute-start | bytes 1572872 | tf_op jit(solution)/shard_map/ppermute | solution.py:265
  120.9 9.4 %collective-permute-start.25 = (bf16[128,2048]{1,0:T(8,128)(2,1)S(1)}, bf16[128,2048]{1,0:T(8,128)(2,1)S(1)}, u32[]{:S(2)}, u32[]{:S(2)}) collective-permute-start(bf16[128,2048]{1,0:T(8,128)(2,1)S(1)} %get-tuple-element.117), channel_id=1, source_target_pairs={{0,1},{1,0},{2,3},{3,2},{4,5},{5,4},{6,7},{7,6},{8,9},{9,8},{10,11... | collective-permute-start | bytes 1572872 | tf_op jit(solution)/shard_map/ppermute | solution.py:268
  121.1 14.4 %collective-permute-start.30 = (bf16[256,1024]{1,0:T(8,128)(2,1)S(1)}, bf16[256,1024]{1,0:T(8,128)(2,1)S(1)}, u32[]{:S(2)}, u32[]{:S(2)}) collective-permute-start(bf16[256,1024]{1,0:T(8,128)(2,1)S(1)} %slice.38), channel_id=1, source_target_pairs={{0,16},{8,24},{16,0},{24,8},{1,17},{9,25},{17,1},{25,9},{2,18},{10... | collective-permute-start | bytes 1572872 | tf_op jit(solution)/shard_map/ppermute | solution.py:271
  122.6 14.1 %collective-permute-start.31 = (bf16[256,1024]{1,0:T(8,128)(2,1)S(1)}, bf16[256,1024]{1,0:T(8,128)(2,1)S(1)}, u32[]{:S(2)}, u32[]{:S(2)}) collective-permute-start(bf16[256,1024]{1,0:T(8,128)(2,1)S(1)} %slice.39), channel_id=1, source_target_pairs={{0,8},{8,0},{16,24},{24,16},{1,9},{9,1},{17,25},{25,17},{2,10},{10... | collective-permute-start | bytes 1572872 | tf_op jit(solution)/shard_map/ppermute | solution.py:271
  130.2 18.9 %collective-permute-start.21 = (bf16[128,4096]{1,0:T(8,128)(2,1)S(1)}, bf16[128,4096]{1,0:T(8,128)(2,1)S(1)}, u32[]{:S(2)}, u32[]{:S(2)}) collective-permute-start(bf16[128,4096]{1,0:T(8,128)(2,1)S(1)} %constant_dynamic-update-slice_fusion.5.mine), channel_id=1, source_target_pairs={{0,1},{1,0},{2,3},{3,2},{4,5},{5,4},{6,7},{7,6},{8,9},{9,8},{10,11... | collective-permute-start | bytes 3145736 | tf_op jit(solution)/shard_map/ppermute | solution.py:268
  130.4 15.4 %collective-permute-start.26 = (bf16[128,2048]{1,0:T(8,128)(2,1)S(1)}, bf16[128,2048]{1,0:T(8,128)(2,1)S(1)}, u32[]{:S(2)}, u32[]{:S(2)}) collective-permute-start(bf16[128,2048]{1,0:T(8,128)(2,1)S(1)} %add_convert_fusion.5), channel_id=1, source_target_pairs={{0,2},{1,3},{2,6},{3,7},{6,4},{7,5},{4,0},{5,1},{8,10},{9,11},{10,... | collective-permute-start | bytes 1572872 | tf_op jit(solution)/shard_map/ppermute | solution.py:265
  137.5 9.2 %collective-permute-start.35 = (bf16[128,2048]{1,0:T(8,128)(2,1)S(1)}, bf16[128,2048]{1,0:T(8,128)(2,1)S(1)}, u32[]{:S(2)}, u32[]{:S(2)}) collective-permute-start(bf16[128,2048]{1,0:T(8,128)(2,1)S(1)} %get-tuple-element.132), channel_id=1, source_target_pairs={{0,1},{1,0},{2,3},{3,2},{4,5},{5,4},{6,7},{7,6},{8,9},{9,8},{10,11... | collective-permute-start | bytes 1572872 | tf_op jit(solution)/shard_map/ppermute | solution.py:268
  146.6 9.1 %collective-permute-start.27 = (bf16[128,2048]{1,0:T(8,128)(2,1)S(1)}, bf16[128,2048]{1,0:T(8,128)(2,1)S(1)}, u32[]{:S(2)}, u32[]{:S(2)}) collective-permute-start(bf16[128,2048]{1,0:T(8,128)(2,1)S(1)} %get-tuple-element.121), channel_id=1, source_target_pairs={{0,1},{1,0},{2,3},{3,2},{4,5},{5,4},{6,7},{7,6},{8,9},{9,8},{10,11... | collective-permute-start | bytes 1572872 | tf_op jit(solution)/shard_map/ppermute | solution.py:268
  146.8 15.7 %collective-permute-start.36 = (bf16[128,2048]{1,0:T(8,128)(2,1)S(1)}, bf16[128,2048]{1,0:T(8,128)(2,1)S(1)}, u32[]{:S(2)}, u32[]{:S(2)}) collective-permute-start(bf16[128,2048]{1,0:T(8,128)(2,1)S(1)} %add_convert_fusion.2), channel_id=1, source_target_pairs={{0,2},{1,3},{2,6},{3,7},{6,4},{7,5},{4,0},{5,1},{8,10},{9,11},{10,... | collective-permute-start | bytes 1572872 | tf_op jit(solution)/shard_map/ppermute | solution.py:265
  148.8 13.7 %collective-permute-start.34 = (bf16[128,2048]{1,0:T(8,128)(2,1)S(1)}, bf16[128,2048]{1,0:T(8,128)(2,1)S(1)}, u32[]{:S(2)}, u32[]{:S(2)}) collective-permute-start(bf16[128,2048]{1,0:T(8,128)(2,1)S(1)} %get-tuple-element.129), channel_id=1, source_target_pairs={{0,1},{1,0},{2,3},{3,2},{4,5},{5,4},{6,7},{7,6},{8,9},{9,8},{10,11... | collective-permute-start | bytes 1572872 | tf_op jit(solution)/shard_map/ppermute | solution.py:268
  154.3 16.0 %collective-permute-start.22 = (bf16[128,2048]{1,0:T(8,128)(2,1)S(1)}, bf16[128,2048]{1,0:T(8,128)(2,1)S(1)}, u32[]{:S(2)}, u32[]{:S(2)}) collective-permute-start(bf16[128,2048]{1,0:T(8,128)(2,1)S(1)} %get-tuple-element.115), channel_id=1, source_target_pairs={{0,1},{1,0},{2,3},{3,2},{4,5},{5,4},{6,7},{7,6},{8,9},{9,8},{10,11... | collective-permute-start | bytes 1572872 | tf_op jit(solution)/shard_map/ppermute | solution.py:268
  155.4 8.8 %copy-start.14 = (bf16[1,1,128,4096]{3,2,1,0:T(8,128)(2,1)S(1)}, bf16[1,1,128,4096]{3,2,1,0:T(8,128)(2,1)}, u32[]{:S(2)}) copy-start(bf16[1,1,128,4096]{3,2,1,0:T(8,128)(2,1)} %param.8) | copy-start | bytes 3145732
  155.4 8.8 %copy-start.16 = (bf16[128,4096]{1,0:T(8,128)(2,1)S(1)}, bf16[128,4096]{1,0:T(8,128)(2,1)}, u32[]{:S(2)}) copy-start(bf16[128,4096]{1,0:T(8,128)(2,1)} %copy-done.15) | copy-start | bytes 3145732
  155.4 19.8 %collective-permute-start.33 = (bf16[128,2048]{1,0:T(8,128)(2,1)S(1)}, bf16[128,2048]{1,0:T(8,128)(2,1)S(1)}, u32[]{:S(2)}, u32[]{:S(2)}) collective-permute-start(bf16[128,2048]{1,0:T(8,128)(2,1)S(1)} %get-tuple-element.127), channel_id=1, source_target_pairs={{0,1},{1,0},{2,3},{3,2},{4,5},{5,4},{6,7},{7,6},{8,9},{9,8},{10,11... | collective-permute-start | bytes 1572872 | tf_op jit(solution)/shard_map/ppermute | solution.py:268
  155.9 17.8 %collective-permute-start.28 = (bf16[128,2048]{1,0:T(8,128)(2,1)S(1)}, bf16[128,2048]{1,0:T(8,128)(2,1)S(1)}, u32[]{:S(2)}, u32[]{:S(2)}) collective-permute-start(bf16[128,2048]{1,0:T(8,128)(2,1)S(1)} %add_convert_fusion.4), channel_id=1, source_target_pairs={{0,2},{1,3},{2,6},{3,7},{6,4},{7,5},{4,0},{5,1},{8,10},{9,11},{10,... | collective-permute-start | bytes 1572872 | tf_op jit(solution)/shard_map/ppermute | solution.py:265
  162.7 22.2 %collective-permute-start.37 = (bf16[128,2048]{1,0:T(8,128)(2,1)S(1)}, bf16[128,2048]{1,0:T(8,128)(2,1)S(1)}, u32[]{:S(2)}, u32[]{:S(2)}) collective-permute-start(bf16[128,2048]{1,0:T(8,128)(2,1)S(1)} %add_convert_fusion.1), channel_id=1, source_target_pairs={{0,2},{1,3},{2,6},{3,7},{6,4},{7,5},{4,0},{5,1},{8,10},{9,11},{10,... | collective-permute-start | bytes 1572872 | tf_op jit(solution)/shard_map/ppermute | solution.py:265
  169.4 17.7 %collective-permute-start.19 = (bf16[128,2048]{1,0:T(8,128)(2,1)S(1)}, bf16[128,2048]{1,0:T(8,128)(2,1)S(1)}, u32[]{:S(2)}, u32[]{:S(2)}) collective-permute-start(bf16[128,2048]{1,0:T(8,128)(2,1)S(1)} %get-tuple-element.112), channel_id=1, source_target_pairs={{0,1},{1,0},{2,3},{3,2},{4,5},{5,4},{6,7},{7,6},{8,9},{9,8},{10,11... | collective-permute-start | bytes 1572872 | tf_op jit(solution)/shard_map/ppermute | solution.py:268
  170.2 16.9 %collective-permute-start.32 = (bf16[128,2048]{1,0:T(8,128)(2,1)S(1)}, bf16[128,2048]{1,0:T(8,128)(2,1)S(1)}, u32[]{:S(2)}, u32[]{:S(2)}) collective-permute-start(bf16[128,2048]{1,0:T(8,128)(2,1)S(1)} %get-tuple-element.125), channel_id=1, source_target_pairs={{0,1},{1,0},{2,3},{3,2},{4,5},{5,4},{6,7},{7,6},{8,9},{9,8},{10,11... | collective-permute-start | bytes 1572872 | tf_op jit(solution)/shard_map/ppermute | solution.py:268
  173.9 22.2 %collective-permute-start.29 = (bf16[128,2048]{1,0:T(8,128)(2,1)S(1)}, bf16[128,2048]{1,0:T(8,128)(2,1)S(1)}, u32[]{:S(2)}, u32[]{:S(2)}) collective-permute-start(bf16[128,2048]{1,0:T(8,128)(2,1)S(1)} %add_convert_fusion.3), channel_id=1, source_target_pairs={{0,2},{1,3},{2,6},{3,7},{6,4},{7,5},{4,0},{5,1},{8,10},{9,11},{10,... | collective-permute-start | bytes 1572872 | tf_op jit(solution)/shard_map/ppermute | solution.py:265
  185.2 21.8 %collective-permute-start.38 = (bf16[128,2048]{1,0:T(8,128)(2,1)S(1)}, bf16[128,2048]{1,0:T(8,128)(2,1)S(1)}, u32[]{:S(2)}, u32[]{:S(2)}) collective-permute-start(bf16[128,2048]{1,0:T(8,128)(2,1)S(1)} %add_convert_fusion), channel_id=1, source_target_pairs={{0,2},{1,3},{2,6},{3,7},{6,4},{7,5},{4,0},{5,1},{8,10},{9,11},{10,... | collective-permute-start | bytes 1572872 | tf_op jit(solution)/shard_map/ppermute | solution.py:265
Sparse Core Ops, SparseCore 0:
  34.9 50.1 all-gather.2
